TPU v7x, 256 devices: a whole 4x4x8 slice. The times are simulated.
256 devices in a mesh: section: 2 (over x_lo), gr: 8 (over y, core), gc: 16 (over x_hi, z).
Axes of the slice: x: 4 (x_hi: 2, x_lo: 2; x = x_hi * 2 + x_lo), y: 4, z: 8, core: 2. Of those that a mesh axis runs over, the one named last changes fastest.
Arguments:
- pair: bfloat16 [2, 512, 512, 128], P(None, 'gr', 'gc'), may hold values from -6 to 6
- single: bfloat16 [2, 512, 384], P(None, 'gr'), may hold values from -6 to 6
- lengths: int32 [2], replicated, may hold values from 256 to 512, as said below
- tri_in: bfloat16 [2, 128, 512], P('section'), may hold values from -0.5 to 0.5
- tri_gate: bfloat16 [2, 128, 128], P('section'), may hold values from -0.5 to 0.5
- tri_out: bfloat16 [2, 128, 128], P('section'), may hold values from -0.5 to 0.5
- pt_in: bfloat16 [2, 128, 1024], P('section'), may hold values from -0.5 to 0.5
- pt_out: bfloat16 [2, 512, 128], P('section'), may hold values from -0.25 to 0.25
- st_in: bfloat16 [2, 384, 3072], P('section'), may hold values from -0.3125 to 0.3125
- st_out: bfloat16 [2, 1536, 384], P('section'), may hold values from -0.15625 to 0.15625
Outputs:
- pair_out: bfloat16 [2, 2, 512, 512, 128], P('section', None, 'gr', 'gc')
- single_out: bfloat16 [2, 2, 512, 384], P('section', None, 'gr')
Inputs may be any that keep to these rules, and one draw needn't show every extreme that they name: `lengths`: each micro-batch's count of real tokens at the start of the crop; some micro-batch is a full crop of 512 and some has exactly half.
All inputs are finite; a program needn't handle non-finite values.
Results may differ from a plain program's by a relative error of at most 0.024.
Values may be sent and summed in bfloat16 or wider, within the bound.
A program may use at most 128 MiB of HBM per device.

v0:
```python
import jax
import jax.numpy as jnp
from jax import lax
from jax.experimental import pallas as pl
from jax.experimental.pallas import tpu as pltpu
from jax.sharding import PartitionSpec as P

MESH = pl.DeviceIdType.MESH
FULL, HALF = 0, 1
BF = jnp.bfloat16
F32 = jnp.float32


def dot(a, b):
    return jnp.dot(a, b, preferred_element_type=F32)


def dot_nt(a, b):
    return lax.dot_general(a, b, (((1,), (1,)), ((), ())), preferred_element_type=F32)


def sigmoid(v):
    return 0.5 + 0.5 * jnp.tanh(0.5 * v)


def norm_lanes(v):
    center = v - jnp.mean(v, axis=-1, keepdims=True)
    spread = jnp.mean(center * center, axis=-1, keepdims=True)
    return center * lax.rsqrt(spread + 1e-05)


def iota(shape, axis):
    return lax.broadcasted_iota(jnp.int32, shape, axis)


def trunk_kernel(
    zin, sin, tin, tgate, tout, pin, pout, st_in, st_out,
    out, sout,
    w_tin, w_gate, w_out, w_pin, w_pout, w_t, st_in_v, st_out_v, sin_next,
    zmid, zlast, normed, stage, settled, perm, order_full, order_half,
    sbuf, rbuf_full, rbuf_half, lm_full, raw_full, all_full, lm_half, raw_half, all_half,
    ts_full, ts_half, tr_full, tr_half,
    fwd_send, fwd_recv, sib_send, sib_recv, back_send, back_recv,
    w_send, w_recv, st_sem, single_send, single_recv, out_send, out_recv,
):
    sec, gr, gc = lax.axis_index("section"), lax.axis_index("gr"), lax.axis_index("gc")
    y, core = lax.shift_right_logical(gr, 1), lax.bitwise_and(gr, 1)
    sy = sec * 4 + y
    me = gc * 8 + sy
    me_half = gc * 4 + sec * 2 + y
    active = jnp.logical_and(y < 2, gc < 8)
    peer = {"section": 1 - sec, "gr": gr, "gc": gc}
    sibling = {"section": sec, "gr": gr + 1 - 2 * core, "gc": gc}

    def place(step):
        to_gc = lax.bitwise_and(gc + step, 15)
        to_sy = lax.bitwise_and(sy + lax.shift_right_logical(step, 4), 7)
        to_sec = lax.shift_right_logical(to_sy, 2)
        to_y = lax.bitwise_and(to_sy, 3)
        return to_gc, to_sy, {"section": to_sec, "gr": to_y * 2 + core, "gc": to_gc}

    st_copies = [
        pltpu.make_async_copy(st_in, st_in_v, st_sem.at[0]),
        pltpu.make_async_copy(st_out, st_out_v, st_sem.at[1]),
    ]
    for copy in st_copies:
        copy.start()

    barrier = pltpu.get_barrier_semaphore()

    def greet(step, carry):
        pl.semaphore_signal(barrier, inc=1, device_id=place(step)[2], device_id_type=MESH)
        return carry

    pl.semaphore_signal(barrier, inc=1, device_id=sibling, device_id_type=MESH)
    lax.fori_loop(1, 128, greet, 0)

    weights = [(tin, w_tin), (tgate, w_gate), (tout, w_out), (pin, w_pin), (pout, w_pout)]
    for own, held in weights:
        held[sec] = own[...]

    from_lane, to_lane = iota((128, 512), 0), iota((128, 512), 1)
    for low in range(4):
        target = (from_lane >> 5) * 128 + low * 32 + (from_lane & 31)
        perm[low] = jnp.where(to_lane == target, 1.0, 0.0).astype(BF)
    o, i = iota((256, 256), 0), iota((256, 256), 1)
    source = (o & 3) * 64 + ((o >> 5) & 1) * 32 + (o >> 6) * 8 + ((o >> 2) & 7)
    order_full[...] = jnp.where(i == source, 1.0, 0.0).astype(BF)
    o, i = iota((128, 128), 0), iota((128, 128), 1)
    source = (o & 3) * 32 + ((o >> 5) & 1) * 16 + (o >> 6) * 8 + ((o >> 2) & 7)
    order_half[...] = jnp.where(i == source, 1.0, 0.0).astype(BF)

    for kind in (FULL, HALF):
        for part in range(4):
            rows = pl.ds(part * 256, 256)
            normed[kind, rows] = norm_lanes(zin[kind, rows].astype(F32)).astype(BF)

    pl.semaphore_wait(barrier, 128)

    def weight_copy(index):
        own, held = weights[index]
        return pltpu.make_async_remote_copy(
            own, held.at[sec], w_send.at[index], w_recv.at[index],
            device_id=peer, device_id_type=MESH,
        )

    weight_copy(0).start()

    def await_weight(block, index):
        @pl.when(sec != block)
        def _():
            held = weights[index][1].at[block]
            pltpu.make_async_copy(held, held, w_recv.at[index]).wait()

    def project(block, kind):
        for part in range(4):
            rows = pl.ds(part * 256, 256)
            p = dot_nt(w_t[...], normed[kind, rows])
            left = sigmoid(p[0:128]) * p[128:256]
            right = sigmoid(p[256:384]) * p[384:512]
            for sub in range(2):
                cols = slice(sub * 128, sub * 128 + 128)
                stage[pl.ds(part * 2 + sub, 128, stride=16), :] = left[:, cols]
                stage[pl.ds(8 + part * 2 + sub, 128, stride=16), :] = right[:, cols]
        for part in range(8):
            values = stage[part * 256 : part * 256 + 256, :].astype(BF)
            sbuf[block, kind, part * 16 : part * 16 + 16] = values.reshape(16, 16, 128)

    def send_forward(block, kind):
        rbuf, slot = (rbuf_full, me) if kind == FULL else (rbuf_half, me_half)

        def send(step, carry):
            to_gc, to_sy, device = place(step)
            pltpu.make_async_remote_copy(
                sbuf.at[block, kind, to_gc * 8 + to_sy], rbuf.at[block, slot],
                fwd_send.at[block, kind], fwd_recv.at[block, kind],
                device_id=device, device_id_type=MESH,
            ).start()
            return carry

        lax.fori_loop(1, 128, send, 0)
        pltpu.make_async_copy(
            sbuf.at[block, kind, me], rbuf.at[block, slot], fwd_recv.at[block, kind]
        ).start()

    def forward(block, kind):
        if kind == FULL:
            project(block, kind)
            send_forward(block, kind)
        else:

            @pl.when(active)
            def _():
                project(block, kind)
                send_forward(block, kind)

    def triangle(block, kind):
        full = kind == FULL
        rbuf, lm, raw, whole, ts, order, groups, tiles = (
            (rbuf_full, lm_full, raw_full, all_full, ts_full, order_full, 4, 8)
            if full
            else (rbuf_half, lm_half, raw_half, all_half, ts_half, order_half, 2, 4)
        )
        depth = groups * 128
        rows = tiles * 8
        landed = rbuf.at[block]
        pltpu.make_async_copy(landed, landed, fwd_recv.at[block, kind]).wait()
        for g in range(groups):
            total = None
            for low in range(4):
                col = g * 4 + low
                block_in = rbuf[block, col * tiles : (col + 1) * tiles].reshape(tiles * 16, 128)
                term = dot(block_in, perm[low])
                total = term if total is None else total + term
            total = total.reshape(tiles, 16, 512)
            left = total[:, 0:8].reshape(rows, 512).astype(BF)
            right = total[:, 8:16].reshape(rows, 512).astype(BF)
            for low in range(4):
                cols = slice(low * 128, low * 128 + 128)
                lm[low * rows : (low + 1) * rows, g * 128 : g * 128 + 128] = left[:, cols]
                raw[low * rows : (low + 1) * rows, g * 128 : g * 128 + 128] = right[:, cols]
        ordered = dot(order[...], raw[...]).astype(BF)
        whole[block, core] = ordered.reshape(tiles // 2, 64, depth)
        mine = whole.at[block, core]
        pltpu.make_async_remote_copy(
            mine, mine, sib_send.at[block, kind], sib_recv.at[block, kind],
            device_id=sibling, device_id_type=MESH,
        ).start()
        other = whole.at[block, 1 - core]
        pltpu.make_async_copy(other, other, sib_recv.at[block, kind]).wait()
        for g in range(groups):
            right = jnp.concatenate(
                [whole[block, 0, g], whole[block, 1, g]], axis=0
            )
            product = dot_nt(lm[...], right).astype(BF)
            total = None
            for low in range(4):
                term = dot(product[low * rows : (low + 1) * rows], perm[low])
                total = term if total is None else total + term
            total = total.astype(BF)
            for low in range(4):
                ts[block, g * 4 + low] = total[:, low * 128 : low * 128 + 128].reshape(
                    tiles, 8, 128
                )

    def send_back(block, kind):
        if kind == FULL:

            def send(step, carry):
                to_gc, to_sy, device = place(step)
                pltpu.make_async_remote_copy(
                    ts_full.at[block, to_gc, to_sy], tr_full.at[block, me],
                    back_send.at[block, kind], back_recv.at[block, kind],
                    device_id=device, device_id_type=MESH,
                ).start()
                return carry

            lax.fori_loop(1, 128, send, 0)
            pltpu.make_async_copy(
                ts_full.at[block, gc, sy], tr_full.at[block, me], back_recv.at[block, kind]
            ).start()
        else:

            def send(step, carry):
                to_gc = lax.bitwise_and(gc + step, 7)
                to_q = lax.bitwise_and(sec * 2 + y + lax.shift_right_logical(step, 3), 3)
                to_sec, to_y = lax.shift_right_logical(to_q, 1), lax.bitwise_and(to_q, 1)
                itself = jnp.logical_and(
                    to_gc == gc, jnp.logical_and(to_sec == sec, to_y == y)
                )

                @pl.when(itself)
                def _():
                    pltpu.make_async_copy(
                        ts_half.at[block, to_gc, to_q], tr_half.at[block, me],
                        back_recv.at[block, kind],
                    ).start()

                @pl.when(jnp.logical_not(itself))
                def _():
                    pltpu.make_async_remote_copy(
                        ts_half.at[block, to_gc, to_q], tr_half.at[block, me],
                        back_send.at[block, kind], back_recv.at[block, kind],
                        device_id={"section": to_sec, "gr": to_y * 2 + core, "gc": to_gc},
                        device_id_type=MESH,
                    ).start()

                return carry

            lax.fori_loop(0, 32, send, 0)

    def finish(block, kind):
        z = zin if block == 0 else zmid
        znext = zmid if block == 0 else zlast
        tr = tr_full if kind == FULL else tr_half
        landed = tr.at[block]
        if kind == FULL:
            pltpu.make_async_copy(landed, landed, back_recv.at[block, kind]).wait()
        else:

            @pl.when(active)
            def _():
                pltpu.make_async_copy(landed, landed, back_recv.at[block, kind]).wait()

            @pl.when(jnp.logical_not(active))
            def _():
                tr[block] = jnp.zeros((128, 8, 128), BF)

        values = tr[block].astype(F32)
        center = values - jnp.mean(values, axis=0, keepdims=True)
        spread = jnp.mean(center * center, axis=0, keepdims=True)
        center = center * lax.rsqrt(spread + 1e-05)
        stage[0:1024, :] = center.reshape(1024, 128)
        for r in range(8):
            tile = stage[pl.ds(r, 128, stride=8), :]
            settled[r * 128 : r * 128 + 128] = tile.T.astype(BF)
        for part in range(4):
            rows = pl.ds(part * 256, 256)
            gate = sigmoid(dot(normed[kind, rows], w_gate[block]))
            update = dot(settled[rows], w_out[block])
            updated = (z[kind, rows].astype(F32) + gate * update).astype(BF)
            updated = updated.astype(F32)
            trans_in = norm_lanes(updated).astype(BF)
            gates = dot(trans_in, w_pin[block, :, 0:512])
            ups = dot(trans_in, w_pin[block, :, 512:1024])
            inner = (gates * sigmoid(gates) * ups).astype(BF)
            done = (updated + dot(inner, w_pout[block])).astype(BF)
            znext[kind, rows] = done
            if block == 0:
                normed[kind, rows] = norm_lanes(done.astype(F32)).astype(BF)

    def deliver(block, kind):
        znext = zmid if block == 0 else zlast

        @pl.when(sec == block)
        def _():
            out[kind, sec] = znext[kind]

        @pl.when(sec != block)
        def _():
            pltpu.make_async_remote_copy(
                znext.at[kind], out.at[kind, sec], out_send.at[kind], out_recv.at[kind],
                device_id=peer, device_id_type=MESH,
            ).start()

    def single(rows_in):
        value = rows_in[...].astype(F32)
        value_in = norm_lanes(value).astype(BF)
        total = value
        for part in range(6):
            cols = part * 256
            gates = dot(value_in, st_in_v[:, cols : cols + 256])
            ups = dot(value_in, st_in_v[:, 1536 + cols : 1536 + cols + 256])
            inner = (gates * sigmoid(gates) * ups).astype(BF)
            total = total + dot(inner, st_out_v[cols : cols + 256])
        sout[...] = total.astype(BF)

    single_copy = pltpu.make_async_remote_copy(
        sout, sin_next, single_send, single_recv, device_id=peer, device_id_type=MESH
    )

    for block in range(2):
        await_weight(block, 0)
        w_t[...] = w_tin[block].astype(F32).T.astype(BF)
        if block == 0:
            forward(block, FULL)
            for index in range(1, 5):
                weight_copy(index).start()
            forward(block, HALF)
        else:
            forward(block, FULL)
            finish(0, HALF)
            deliver(0, HALF)
            forward(block, HALF)

        @pl.when(sec == block)
        def _():
            if block == 0:
                for copy in st_copies:
                    copy.wait()
                single(sin)
                single_copy.start()
            else:
                for copy in st_copies:
                    copy.wait()
                single_copy.wait_recv()
                single(sin_next)

        triangle(block, FULL)
        send_back(block, FULL)
        triangle(block, HALF)
        send_back(block, HALF)
        for index in range(1, 5):
            await_weight(block, index)
        finish(block, FULL)
        deliver(block, FULL)
    finish(1, HALF)
    deliver(1, HALF)

    for block in range(2):
        for kind in (FULL, HALF):
            sent = rbuf_full.at[block, pl.ds(0, 127)]
            wait_sent = pltpu.make_async_copy(sent, sent, fwd_send.at[block, kind])
            if kind == FULL:
                wait_sent.wait()
            else:
                pl.when(active)(wait_sent.wait)
            whole = all_full if kind == FULL else all_half
            mine = whole.at[block, core]
            pltpu.make_async_copy(mine, mine, sib_send.at[block, kind]).wait()
            if kind == FULL:
                sent = tr_full.at[block, pl.ds(0, 127)]
                pltpu.make_async_copy(sent, sent, back_send.at[block, kind]).wait()
            else:

                @pl.when(active)
                def _():
                    sent = tr_half.at[block, pl.ds(0, 31)]
                    pltpu.make_async_copy(sent, sent, back_send.at[block, kind]).wait()

                @pl.when(jnp.logical_not(active))
                def _():
                    sent = tr_half.at[block, pl.ds(0, 32)]
                    pltpu.make_async_copy(sent, sent, back_send.at[block, kind]).wait()

    for index in range(5):
        weight_copy(index).wait_send()
    pl.when(sec == 0)(single_copy.wait_send)
    for kind in (FULL, HALF):
        given = zlast.at[kind]
        pltpu.make_async_copy(given, given, out_send.at[kind]).wait()
        taken = out.at[kind, 1 - sec]
        pltpu.make_async_copy(taken, taken, out_recv.at[kind]).wait()


def trunk(zin, sin, tin, tgate, tout, pin, pout, st_in, st_out):
    vmem = pl.BlockSpec(memory_space=pltpu.VMEM)
    anywhere = pl.BlockSpec(memory_space=pl.ANY)
    dma = pltpu.SemaphoreType.DMA
    return pl.pallas_call(
        trunk_kernel,
        out_shape=(
            jax.ShapeDtypeStruct((2, 2, 1024, 128), BF),
            jax.ShapeDtypeStruct((128, 384), BF),
        ),
        in_specs=[vmem] * 7 + [anywhere] * 2,
        out_specs=(vmem, vmem),
        scratch_shapes=[
            pltpu.VMEM((2, 128, 512), BF),
            pltpu.VMEM((2, 128, 128), BF),
            pltpu.VMEM((2, 128, 128), BF),
            pltpu.VMEM((2, 128, 1024), BF),
            pltpu.VMEM((2, 512, 128), BF),
            pltpu.VMEM((512, 128), BF),
            pltpu.VMEM((384, 3072), BF),
            pltpu.VMEM((1536, 384), BF),
            pltpu.VMEM((128, 384), BF),
            pltpu.VMEM((2, 1024, 128), BF),
            pltpu.VMEM((2, 1024, 128), BF),
            pltpu.VMEM((2, 1024, 128), BF),
            pltpu.VMEM((2048, 128), F32),
            pltpu.VMEM((1024, 128), BF),
            pltpu.VMEM((4, 128, 512), BF),
            pltpu.VMEM((256, 256), BF),
            pltpu.VMEM((128, 128), BF),
            pltpu.VMEM((2, 2, 128, 16, 128), BF),
            pltpu.VMEM((2, 128, 16, 128), BF),
            pltpu.VMEM((2, 32, 16, 128), BF),
            pltpu.VMEM((256, 512), BF),
            pltpu.VMEM((256, 512), BF),
            pltpu.VMEM((2, 2, 4, 64, 512), BF),
            pltpu.VMEM((128, 256), BF),
            pltpu.VMEM((128, 256), BF),
            pltpu.VMEM((2, 2, 2, 64, 256), BF),
            pltpu.VMEM((2, 16, 8, 8, 128), BF),
            pltpu.VMEM((2, 8, 4, 8, 128), BF),
            pltpu.VMEM((2, 128, 8, 128), BF),
            pltpu.VMEM((2, 128, 8, 128), BF),
            dma((2, 2)),
            dma((2, 2)),
            dma((2, 2)),
            dma((2, 2)),
            dma((2, 2)),
            dma((2, 2)),
            dma((5,)),
            dma((5,)),
            dma((2,)),
            dma,
            dma,
            dma((2,)),
            dma((2,)),
        ],
        compiler_params=pltpu.CompilerParams(
            collective_id=0, has_side_effects=True, vmem_limit_bytes=56 << 20
        ),
    )(zin, sin, tin, tgate, tout, pin, pout, st_in, st_out)


def on_device(pair, single, lengths, tri_in, tri_gate, tri_out, pt_in, pt_out, st_in, st_out):
    first_full = lengths[0] > lengths[1]
    start = lax.axis_index("section") * 32
    part = lax.dynamic_slice_in_dim(pair, start, 32, 1).reshape(2, 1024, 128)
    zin = jnp.where(first_full, part, part[::-1])
    out, sout = trunk(
        zin,
        single.reshape(128, 384),
        tri_in[0], tri_gate[0], tri_out[0], pt_in[0], pt_out[0], st_in[0], st_out[0],
    )
    out = out.reshape(2, 64, 32, 128)
    out = jnp.where(first_full, out, out[::-1])
    return out[None], sout.reshape(1, 2, 64, 384)


def solution(mesh):
    section = P("section", None, None)
    in_specs = (P(None, "gr", "gc", None), P(None, "gr", None), P()) + (section,) * 7
    out_specs = (P("section", None, "gr", "gc", None), P("section", None, "gr", None))
    return jax.shard_map(
        on_device, mesh=mesh, in_specs=in_specs, out_specs=out_specs, check_vma=False
    )
```

profile of v0, /device:TPU:2, one launch (start us, length us, event | category | flops | bytes accessed | tf_op | source)
XLA Modules:
  0.0 115.0 jit_solution(14273099410969520556)
XLA Ops:
  0.6 0.0 copy-start
  0.6 1.3 %fusion.1 = (s32[1]{0:T(128)}, s32[1]{0:T(128)}) fusion(s32[2]{0:T(128)} %param.12), kind=kLoop, calls=%fused_computation.4 | loop fusion | bytes 16 | tf_op jit(solution)/shard_map/slice | solution.py:460
  3.3 0.0 copy-done
  3.4 0.9 reverse_select_fusion.1.zin
  4.3 106.4 %shard_map.113 = (bf16[2,2,1024,128]{3,2,1,0:T(8,128)(2,1)}, bf16[128,384]{1,0:T(8,128)(2,1)}) custom-call(bf16[2,1024,128]{2,1,0:T(8,128)(2,1)} %reverse_select_fusion.1.zin, bf16[128,384]{1,0:T(8,128)(2,1)} %bitcast.22, bf16[128,512]{1,0:T(8,128)(2,1)} %bitcast.19, bf16[128,128]{1,0:T(8,128)(2,1)} %bitcast.23, bf16[128,128]{1,0:T(8,128)(2,1)} %bitcast.24, ...), custom_call_target="tpu_custom_call" | custom-call | tf_op jit(solution)/shard_map/pallas_call | solution.py:400
  110.7 2.8 %fusion = bf16[1,2,64,32,128]{4,3,2,1,0:T(8,128)(2,1)} fusion(bf16[2,64,32,128]{3,2,1,0:T(8,128)(2,1)} %bitcast.17, pred[]{:T(512)} %bitcast), kind=kLoop, calls=%fused_computation.1 | loop fusion | flops 524288 | bytes 2097153 | tf_op jit(solution)/shard_map/broadcast_in_dim | solution.py:471
  113.5 1.5 %copy.13 = bf16[1,2,64,384]{3,2,1,0:T(8,128)(2,1)} copy(bf16[1,2,64,384]{3,2,1,0:T(8,128)(2,1)} %bitcast.21) | data formatting | bytes 196608
  (1 shorter events, 0.0 us)
Async XLA Ops:
  0.6 2.7 %copy-start = (bf16[2,64,32,128]{3,2,1,0:T(8,128)(2,1)S(1)}, bf16[2,64,32,128]{3,2,1,0:T(8,128)(2,1)}, u32[]{:S(2)}) copy-start(bf16[2,64,32,128]{3,2,1,0:T(8,128)(2,1)} %param.10) | copy-start | bytes 3145732
where the time goes:
time: 115 us
  Pallas kernels  106 us (92%)
  other arithmetic  3.71 us (3%)
  local copies, waits for them, and re-layouts  2.94 us (3%)
  between operations  1.97 us (2%)
    pallas_call x1, Pallas kernels, trunk(): pl.pallas_call(trunk_kernel, out_shape=(jax.ShapeDtypeStruct((2, 2, 1024,...  106 us
    broadcast_in_dim x1, other arithmetic, on_device(): return (out[None], sout.reshape(1, 2, 64, 384))  2.81 us

commit v1 on v0

--- a/solution.py
+++ b/solution.py
@@ -34,14 +34,14 @@
 
 
 def trunk_kernel(
-    zin, sin, tin, tgate, tout, pin, pout, st_in, st_out,
+    lengths, pair, sin, tin, tgate, tout, pin, pout, st_in, st_out,
     out, sout,
     w_tin, w_gate, w_out, w_pin, w_pout, w_t, st_in_v, st_out_v, sin_next,
-    zmid, zlast, normed, stage, settled, perm, order_full, order_half,
+    zin, zout, normed, stage, settled, perm, order_full, order_half,
     sbuf, rbuf_full, rbuf_half, lm_full, raw_full, all_full, lm_half, raw_half, all_half,
     ts_full, ts_half, tr_full, tr_half,
     fwd_send, fwd_recv, sib_send, sib_recv, back_send, back_recv,
-    w_send, w_recv, st_sem, single_send, single_recv, out_send, out_recv,
+    met, w_send, w_recv, st_sem, single_send, single_recv, out_send, out_recv,
 ):
     sec, gr, gc = lax.axis_index("section"), lax.axis_index("gr"), lax.axis_index("gc")
     y, core = lax.shift_right_logical(gr, 1), lax.bitwise_and(gr, 1)
@@ -68,16 +68,38 @@
 
     barrier = pltpu.get_barrier_semaphore()
 
-    def greet(step, carry):
-        pl.semaphore_signal(barrier, inc=1, device_id=place(step)[2], device_id_type=MESH)
-        return carry
+    def greet_line(semaphore):
+        def greet(step, carry):
+            to_gc = lax.bitwise_and(gc + step, 15)
+            pl.semaphore_signal(
+                semaphore, inc=1, device_id={"section": sec, "gr": gr, "gc": to_gc},
+                device_id_type=MESH,
+            )
+            return carry
+
+        lax.fori_loop(1, 16, greet, 0)
 
     pl.semaphore_signal(barrier, inc=1, device_id=sibling, device_id_type=MESH)
-    lax.fori_loop(1, 128, greet, 0)
+    for step in range(1, 8):
+        pl.semaphore_signal(
+            barrier, inc=1, device_id=place(step * 16)[2], device_id_type=MESH
+        )
+    greet_line(barrier)
 
     weights = [(tin, w_tin), (tgate, w_gate), (tout, w_out), (pin, w_pin), (pout, w_pout)]
     for own, held in weights:
         held[sec] = own[...]
+
+    def weight_copy(index):
+        own, held = weights[index]
+        return pltpu.make_async_remote_copy(
+            own, held.at[sec], w_send.at[index], w_recv.at[index],
+            device_id=peer, device_id_type=MESH,
+        )
+
+    pl.semaphore_wait(barrier, 23)
+    weight_copy(0).start()
+    greet_line(met)
 
     from_lane, to_lane = iota((128, 512), 0), iota((128, 512), 1)
     for low in range(4):
@@ -90,21 +112,15 @@
     source = (o & 3) * 32 + ((o >> 5) & 1) * 16 + (o >> 6) * 8 + ((o >> 2) & 7)
     order_half[...] = jnp.where(i == source, 1.0, 0.0).astype(BF)
 
-    for kind in (FULL, HALF):
+    first = jnp.where(lengths[0] > lengths[1], 0, 1)
+    for kind, crop in ((FULL, first), (HALF, 1 - first)):
         for part in range(4):
             rows = pl.ds(part * 256, 256)
-            normed[kind, rows] = norm_lanes(zin[kind, rows].astype(F32)).astype(BF)
-
-    pl.semaphore_wait(barrier, 128)
-
-    def weight_copy(index):
-        own, held = weights[index]
-        return pltpu.make_async_remote_copy(
-            own, held.at[sec], w_send.at[index], w_recv.at[index],
-            device_id=peer, device_id_type=MESH,
-        )
-
-    weight_copy(0).start()
+            z = pair[crop, pl.ds(sec * 32 + part * 8, 8)].reshape(256, 128)
+            zin[kind, rows] = z
+            normed[kind, rows] = norm_lanes(z.astype(F32)).astype(BF)
+
+    pl.semaphore_wait(met, 15)
 
     def await_weight(block, index):
         @pl.when(sec != block)
@@ -250,8 +266,7 @@
             lax.fori_loop(0, 32, send, 0)
 
     def finish(block, kind):
-        z = zin if block == 0 else zmid
-        znext = zmid if block == 0 else zlast
+        z = zin if block == 0 else zout.at[0]
         tr = tr_full if kind == FULL else tr_half
         landed = tr.at[block]
         if kind == FULL:
@@ -285,21 +300,24 @@
             ups = dot(trans_in, w_pin[block, :, 512:1024])
             inner = (gates * sigmoid(gates) * ups).astype(BF)
             done = (updated + dot(inner, w_pout[block])).astype(BF)
-            znext[kind, rows] = done
+            zout[block, kind, rows] = done
             if block == 0:
                 normed[kind, rows] = norm_lanes(done.astype(F32)).astype(BF)
-
-    def deliver(block, kind):
-        znext = zmid if block == 0 else zlast
+            else:
+                deliver(block, kind, part, 1)
+
+    def deliver(block, kind, part=0, parts=4):
+        rows = pl.ds(part * 256, parts * 256)
 
         @pl.when(sec == block)
         def _():
-            out[kind, sec] = znext[kind]
+            out[kind, sec, rows] = zout[block, kind, rows]
 
         @pl.when(sec != block)
         def _():
             pltpu.make_async_remote_copy(
-                znext.at[kind], out.at[kind, sec], out_send.at[kind], out_recv.at[kind],
+                zout.at[block, kind, rows], out.at[kind, sec, rows],
+                out_send.at[kind], out_recv.at[kind],
                 device_id=peer, device_id_type=MESH,
             ).start()
 
@@ -319,81 +337,101 @@
         sout, sin_next, single_send, single_recv, device_id=peer, device_id_type=MESH
     )
 
-    for block in range(2):
+    def start_block(block):
         await_weight(block, 0)
         w_t[...] = w_tin[block].astype(F32).T.astype(BF)
-        if block == 0:
-            forward(block, FULL)
-            for index in range(1, 5):
-                weight_copy(index).start()
-            forward(block, HALF)
-        else:
-            forward(block, FULL)
-            finish(0, HALF)
-            deliver(0, HALF)
-            forward(block, HALF)
-
+
+    def more_weights():
+        for index in range(1, 5):
+            weight_copy(index).start()
+
+    def rest_weights(block):
+        for index in range(1, 5):
+            await_weight(block, index)
+
+    def single_turn(block):
         @pl.when(sec == block)
         def _():
+            for copy in st_copies:
+                copy.wait()
             if block == 0:
-                for copy in st_copies:
-                    copy.wait()
                 single(sin)
                 single_copy.start()
             else:
-                for copy in st_copies:
-                    copy.wait()
                 single_copy.wait_recv()
                 single(sin_next)
 
-        triangle(block, FULL)
-        send_back(block, FULL)
-        triangle(block, HALF)
-        send_back(block, HALF)
-        for index in range(1, 5):
-            await_weight(block, index)
-        finish(block, FULL)
-        deliver(block, FULL)
+    start_block(0)
+    forward(0, FULL)
+    more_weights()
+    forward(0, HALF)
+    single_turn(0)
+    triangle(0, FULL)
+    send_back(0, FULL)
+    triangle(0, HALF)
+    send_back(0, HALF)
+    rest_weights(0)
+    finish(0, FULL)
+    start_block(1)
+    forward(1, FULL)
+    deliver(0, FULL)
+    finish(0, HALF)
+    forward(1, HALF)
+    deliver(0, HALF)
+    single_turn(1)
+    triangle(1, FULL)
+    send_back(1, FULL)
+    triangle(1, HALF)
+    send_back(1, HALF)
+    rest_weights(1)
+    finish(1, FULL)
     finish(1, HALF)
-    deliver(1, HALF)
-
-    for block in range(2):
-        for kind in (FULL, HALF):
-            sent = rbuf_full.at[block, pl.ds(0, 127)]
-            wait_sent = pltpu.make_async_copy(sent, sent, fwd_send.at[block, kind])
-            if kind == FULL:
-                wait_sent.wait()
-            else:
-                pl.when(active)(wait_sent.wait)
-            whole = all_full if kind == FULL else all_half
-            mine = whole.at[block, core]
-            pltpu.make_async_copy(mine, mine, sib_send.at[block, kind]).wait()
-            if kind == FULL:
-                sent = tr_full.at[block, pl.ds(0, 127)]
-                pltpu.make_async_copy(sent, sent, back_send.at[block, kind]).wait()
-            else:
-
-                @pl.when(active)
-                def _():
-                    sent = tr_half.at[block, pl.ds(0, 31)]
-                    pltpu.make_async_copy(sent, sent, back_send.at[block, kind]).wait()
-
-                @pl.when(jnp.logical_not(active))
-                def _():
-                    sent = tr_half.at[block, pl.ds(0, 32)]
-                    pltpu.make_async_copy(sent, sent, back_send.at[block, kind]).wait()
-
-    for index in range(5):
-        weight_copy(index).wait_send()
-    pl.when(sec == 0)(single_copy.wait_send)
-    for kind in (FULL, HALF):
-        given = zlast.at[kind]
+
+    def end_forward(block, kind):
+        sent = rbuf_full.at[block, pl.ds(0, 127)]
+        copy = pltpu.make_async_copy(sent, sent, fwd_send.at[block, kind])
+        if kind == FULL:
+            copy.wait()
+        else:
+            pl.when(active)(copy.wait)
+
+    def end_triangle(block, kind):
+        mine = (all_full if kind == FULL else all_half).at[block, core]
+        pltpu.make_async_copy(mine, mine, sib_send.at[block, kind]).wait()
+
+    def end_back(block, kind):
+        def wait(count):
+            sent = tr_full.at[block, pl.ds(0, count)]
+            pltpu.make_async_copy(sent, sent, back_send.at[block, kind]).wait()
+
+        if kind == FULL:
+            wait(127)
+        else:
+            pl.when(active)(lambda: wait(31))
+            pl.when(jnp.logical_not(active))(lambda: wait(32))
+
+    def end_rest():
+        for index in range(5):
+            weight_copy(index).wait_send()
+        pl.when(sec == 0)(single_copy.wait_send)
+
+    def end_deliver(kind):
+        given = zout.at[0, kind]
         pltpu.make_async_copy(given, given, out_send.at[kind]).wait()
         taken = out.at[kind, 1 - sec]
         pltpu.make_async_copy(taken, taken, out_recv.at[kind]).wait()
 
-
-def trunk(zin, sin, tin, tgate, tout, pin, pout, st_in, st_out):
+    for block in range(2):
+        for kind in (FULL, HALF):
+            end_forward(block, kind)
+            end_triangle(block, kind)
+            end_back(block, kind)
+    end_rest()
+    end_deliver(FULL)
+    end_deliver(HALF)
+
+
+def trunk(lengths, pair, sin, tin, tgate, tout, pin, pout, st_in, st_out):
     vmem = pl.BlockSpec(memory_space=pltpu.VMEM)
     anywhere = pl.BlockSpec(memory_space=pl.ANY)
     dma = pltpu.SemaphoreType.DMA
@@ -403,7 +441,7 @@
             jax.ShapeDtypeStruct((2, 2, 1024, 128), BF),
             jax.ShapeDtypeStruct((128, 384), BF),
         ),
-        in_specs=[vmem] * 7 + [anywhere] * 2,
+        in_specs=[pl.BlockSpec(memory_space=pltpu.SMEM)] + [vmem] * 7 + [anywhere] * 2,
         out_specs=(vmem, vmem),
         scratch_shapes=[
             pltpu.VMEM((2, 128, 512), BF),
@@ -416,7 +454,7 @@
             pltpu.VMEM((1536, 384), BF),
             pltpu.VMEM((128, 384), BF),
             pltpu.VMEM((2, 1024, 128), BF),
-            pltpu.VMEM((2, 1024, 128), BF),
+            pltpu.VMEM((2, 2, 1024, 128), BF),
             pltpu.VMEM((2, 1024, 128), BF),
             pltpu.VMEM((2048, 128), F32),
             pltpu.VMEM((1024, 128), BF),
@@ -442,6 +480,7 @@
             dma((2, 2)),
             dma((2, 2)),
             dma((2, 2)),
+            pltpu.SemaphoreType.REGULAR,
             dma((5,)),
             dma((5,)),
             dma((2,)),
@@ -453,22 +492,46 @@
         compiler_params=pltpu.CompilerParams(
             collective_id=0, has_side_effects=True, vmem_limit_bytes=56 << 20
         ),
-    )(zin, sin, tin, tgate, tout, pin, pout, st_in, st_out)
+    )(lengths, pair, sin, tin, tgate, tout, pin, pout, st_in, st_out)
+
+
+def restore_kernel(lengths, staged, staged_single, out, sout, sems):
+    first = jnp.where(lengths[0] > lengths[1], 0, 1)
+    copies = [
+        pltpu.make_async_copy(staged.at[micro ^ first, half], out.at[0, micro, half], sems.at[micro, half])
+        for micro in range(2)
+        for half in range(2)
+    ]
+    copies.append(pltpu.make_async_copy(staged_single, sout, sems.at[2, 0]))
+    for copy in copies:
+        copy.start()
+    for copy in copies:
+        copy.wait()
+
+
+def restore(lengths, staged, staged_single):
+    anywhere = pl.BlockSpec(memory_space=pl.ANY)
+    return pl.pallas_call(
+        restore_kernel,
+        out_shape=(
+            jax.ShapeDtypeStruct((1, 2, 2, 1024, 128), BF),
+            jax.ShapeDtypeStruct((128, 384), BF),
+        ),
+        in_specs=[pl.BlockSpec(memory_space=pltpu.SMEM), anywhere, anywhere],
+        out_specs=(anywhere, anywhere),
+        scratch_shapes=[pltpu.SemaphoreType.DMA((3, 2))],
+    )(lengths, staged, staged_single)
 
 
 def on_device(pair, single, lengths, tri_in, tri_gate, tri_out, pt_in, pt_out, st_in, st_out):
-    first_full = lengths[0] > lengths[1]
-    start = lax.axis_index("section") * 32
-    part = lax.dynamic_slice_in_dim(pair, start, 32, 1).reshape(2, 1024, 128)
-    zin = jnp.where(first_full, part, part[::-1])
-    out, sout = trunk(
-        zin,
+    staged, staged_single = trunk(
+        lengths,
+        pair,
         single.reshape(128, 384),
         tri_in[0], tri_gate[0], tri_out[0], pt_in[0], pt_out[0], st_in[0], st_out[0],
     )
-    out = out.reshape(2, 64, 32, 128)
-    out = jnp.where(first_full, out, out[::-1])
-    return out[None], sout.reshape(1, 2, 64, 384)
+    out, sout = restore(lengths, staged, staged_single)
+    return out.reshape(1, 2, 64, 32, 128), sout.reshape(1, 2, 64, 384)
 
 
 def solution(mesh):

time: 115 us -> 137 us (1.19)
  Pallas kernels: 106 us -> 135 us
  other arithmetic: 3.71 us -> 0 us
  local copies, waits for them, and re-layouts: 2.94 us -> 0 us
    pallas_call x0 -> x1, Pallas kernels: none -> 36.6 us  [restore(): pl.pallas_call(restore_kernel, out_shape=(jax.ShapeDtypeStruct((1, 2, 2,...]
    pallas_call x1, Pallas kernels: 106 us -> 98.9 us  [trunk(): pl.pallas_call(trunk_kernel, out_shape=(jax.ShapeDtypeStruct((2, 2, 1024,...]
    broadcast_in_dim x1 -> x0, other arithmetic: 2.81 us -> none  [on_device(): return (out[None], sout.reshape(1, 2, 64, 384))]
    unnamed x3 -> x0, local copies, waits for them, and re-layouts: 1.55 us -> none
where the time goes in v1:
time: 137 us; the launch traced here: 136 us
  Pallas kernels  135 us (99%)
    pallas_call x1, Pallas kernels, trunk(): pl.pallas_call(trunk_kernel, out_shape=(jax.ShapeDtypeStruct((2, 2, 1024,...  98.9 us
    pallas_call x1, Pallas kernels, restore(): pl.pallas_call(restore_kernel, out_shape=(jax.ShapeDtypeStruct((1, 2, 2,...  36.6 us

profile of v1, /device:TPU:2, one launch (start us, length us, event | category | flops | bytes accessed | tf_op | source)
XLA Modules:
  0.0 136.2 jit_solution(1855800534357645636)
XLA Ops:
  0.6 98.9 %shard_map.113 = (bf16[2,2,1024,128]{3,2,1,0:T(8,128)(2,1)}, bf16[128,384]{1,0:T(8,128)(2,1)}) custom-call(s32[2]{0:T(128)} %lengths.3, bf16[2,64,32,128]{3,2,1,0:T(8,128)(2,1)} %pair.1, bf16[128,384]{1,0:T(8,128)(2,1)} %bitcast.15, bf16[128,512]{1,0:T(8,128)(2,1)} %bitcast.13, bf16[128,128]{1,0:T(8,128)(2,1)} %bitcast.16, bf16[128,128]{1,0:T(8,128)(2,1)} %bitcast.17, ...), custom_call_target="tpu_custom_call" | custom-call | tf_op jit(solution)/shard_map/pallas_call | solution.py:438
  99.5 36.6 %shard_map.114 = (bf16[1,2,2,1024,128]{4,3,2,1,0:T(8,128)(2,1)}, bf16[128,384]{1,0:T(8,128)(2,1)}) custom-call(s32[2]{0:T(128)} %lengths.3, bf16[2,2,1024,128]{3,2,1,0:T(8,128)(2,1)} %get-tuple-element.6.staged, bf16[128,384]{1,0:T(8,128)(2,1)} %get-tuple-element.7.staged_single), custom_call_target="tpu_custom_call" | custom-call | tf_op jit(solution)/shard_map/pallas_call | solution.py:514

commit v2 on v1

--- a/solution.py
+++ b/solution.py
@@ -27,6 +27,17 @@
     center = v - jnp.mean(v, axis=-1, keepdims=True)
     spread = jnp.mean(center * center, axis=-1, keepdims=True)
     return center * lax.rsqrt(spread + 1e-05)
+
+
+def norm_pair(v, mean_of):
+    center = v.astype(F32) - dot(v, mean_of)
+    spread = dot((center * center).astype(BF), mean_of)
+    return (center * lax.rsqrt(spread + 1e-05)).astype(BF)
+
+
+def silu_times(gates, ups):
+    half = 0.5 * gates
+    return ((half + half * jnp.tanh(half)) * ups).astype(BF)
 
 
 def iota(shape, axis):
@@ -40,14 +51,16 @@
     zin, zout, normed, stage, settled, perm, order_full, order_half,
     sbuf, rbuf_full, rbuf_half, lm_full, raw_full, all_full, lm_half, raw_half, all_half,
     ts_full, ts_half, tr_full, tr_half,
-    fwd_send, fwd_recv, sib_send, sib_recv, back_send, back_recv,
+    relayed, relay_send, relay_recv, fwd_send, fwd_recv, sib_send, sib_recv, back_send, back_recv,
     met, w_send, w_recv, st_sem, single_send, single_recv, out_send, out_recv,
 ):
     sec, gr, gc = lax.axis_index("section"), lax.axis_index("gr"), lax.axis_index("gc")
     y, core = lax.shift_right_logical(gr, 1), lax.bitwise_and(gr, 1)
     sy = sec * 4 + y
-    me = gc * 8 + sy
-    me_half = gc * 4 + sec * 2 + y
+    x_hi, z_at = lax.shift_right_logical(gc, 3), lax.bitwise_and(gc, 7)
+    plane = x_hi * 8 + sy
+    channel = plane * 8 + z_at
+    slot = gc * 8 + sy
     active = jnp.logical_and(y < 2, gc < 8)
     peer = {"section": 1 - sec, "gr": gr, "gc": gc}
     sibling = {"section": sec, "gr": gr + 1 - 2 * core, "gc": gc}
@@ -58,6 +71,10 @@
         to_sec = lax.shift_right_logical(to_sy, 2)
         to_y = lax.bitwise_and(to_sy, 3)
         return to_gc, to_sy, {"section": to_sec, "gr": to_y * 2 + core, "gc": to_gc}
+
+    def channel_of(at_gc, at_sy):
+        at_plane = lax.shift_right_logical(at_gc, 3) * 8 + at_sy
+        return at_plane * 8 + lax.bitwise_and(at_gc, 7)
 
     st_copies = [
         pltpu.make_async_copy(st_in, st_in_v, st_sem.at[0]),
@@ -112,13 +129,14 @@
     source = (o & 3) * 32 + ((o >> 5) & 1) * 16 + (o >> 6) * 8 + ((o >> 2) & 7)
     order_half[...] = jnp.where(i == source, 1.0, 0.0).astype(BF)
 
+    mean_of = jnp.full((128, 128), 1 / 128, BF)
     first = jnp.where(lengths[0] > lengths[1], 0, 1)
     for kind, crop in ((FULL, first), (HALF, 1 - first)):
         for part in range(4):
             rows = pl.ds(part * 256, 256)
             z = pair[crop, pl.ds(sec * 32 + part * 8, 8)].reshape(256, 128)
             zin[kind, rows] = z
-            normed[kind, rows] = norm_lanes(z.astype(F32)).astype(BF)
+            normed[kind, rows] = norm_pair(z, mean_of)
 
     pl.semaphore_wait(met, 15)
 
@@ -142,42 +160,76 @@
             values = stage[part * 256 : part * 256 + 256, :].astype(BF)
             sbuf[block, kind, part * 16 : part * 16 + 16] = values.reshape(16, 16, 128)
 
-    def send_forward(block, kind):
-        rbuf, slot = (rbuf_full, me) if kind == FULL else (rbuf_half, me_half)
-
+    def send_full(block, begin, end):
         def send(step, carry):
             to_gc, to_sy, device = place(step)
             pltpu.make_async_remote_copy(
-                sbuf.at[block, kind, to_gc * 8 + to_sy], rbuf.at[block, slot],
-                fwd_send.at[block, kind], fwd_recv.at[block, kind],
+                sbuf.at[block, FULL, channel_of(to_gc, to_sy)], rbuf_full.at[block, slot],
+                fwd_send.at[block, FULL], fwd_recv.at[block, FULL],
                 device_id=device, device_id_type=MESH,
             ).start()
             return carry
 
-        lax.fori_loop(1, 128, send, 0)
+        lax.fori_loop(begin, end, send, 0)
+        if begin == 1:
+            pltpu.make_async_copy(
+                sbuf.at[block, FULL, channel], rbuf_full.at[block, slot],
+                fwd_recv.at[block, FULL],
+            ).start()
+
+    def send_half(block):
+        source = sec * 2 + y
+        for step in range(1, 16):
+            to_plane = lax.bitwise_and(plane + step, 15)
+            to_sy = lax.bitwise_and(to_plane, 7)
+            pltpu.make_async_remote_copy(
+                sbuf.at[block, HALF, pl.ds(to_plane * 8, 8)], relayed.at[block, source],
+                relay_send.at[block], relay_recv.at[block],
+                device_id={
+                    "section": lax.shift_right_logical(to_sy, 2),
+                    "gr": lax.bitwise_and(to_sy, 3) * 2 + core,
+                    "gc": lax.shift_right_logical(to_plane, 3) * 8 + z_at,
+                },
+                device_id_type=MESH,
+            ).start()
         pltpu.make_async_copy(
-            sbuf.at[block, kind, me], rbuf.at[block, slot], fwd_recv.at[block, kind]
+            sbuf.at[block, HALF, pl.ds(plane * 8, 8)], relayed.at[block, source],
+            relay_recv.at[block],
         ).start()
+
+    def relay(block):
+        landed = relayed.at[block]
+        pltpu.make_async_copy(landed, landed, relay_recv.at[block]).wait()
+        at = rbuf_half.at[block, pl.ds(z_at * 4, 4)]
+        for step in range(1, 8):
+            to_z = lax.bitwise_and(z_at + step, 7)
+            pltpu.make_async_remote_copy(
+                relayed.at[block, :, to_z], at, fwd_send.at[block, HALF], fwd_recv.at[block, HALF],
+                device_id={"section": sec, "gr": gr, "gc": x_hi * 8 + to_z},
+                device_id_type=MESH,
+            ).start()
+        pltpu.make_async_copy(relayed.at[block, :, z_at], at, fwd_recv.at[block, HALF]).start()
 
     def forward(block, kind):
         if kind == FULL:
-            project(block, kind)
-            send_forward(block, kind)
+            project(block, FULL)
+            send_full(block, 1, 64)
+            relay(block)
+            send_full(block, 64, 128)
         else:
 
             @pl.when(active)
             def _():
-                project(block, kind)
-                send_forward(block, kind)
-
-    def triangle(block, kind):
-        full = kind == FULL
-        rbuf, lm, raw, whole, ts, order, groups, tiles = (
-            (rbuf_full, lm_full, raw_full, all_full, ts_full, order_full, 4, 8)
-            if full
-            else (rbuf_half, lm_half, raw_half, all_half, ts_half, order_half, 2, 4)
-        )
-        depth = groups * 128
+                project(block, HALF)
+                send_half(block)
+
+    def parts_of(kind):
+        if kind == FULL:
+            return rbuf_full, lm_full, raw_full, all_full, ts_full, tr_full, order_full, 4, 8
+        return rbuf_half, lm_half, raw_half, all_half, ts_half, tr_half, order_half, 2, 4
+
+    def triangle_in(block, kind):
+        rbuf, lm, raw, whole, ts, tr, order, groups, tiles = parts_of(kind)
         rows = tiles * 8
         landed = rbuf.at[block]
         pltpu.make_async_copy(landed, landed, fwd_recv.at[block, kind]).wait()
@@ -191,23 +243,31 @@
             total = total.reshape(tiles, 16, 512)
             left = total[:, 0:8].reshape(rows, 512).astype(BF)
             right = total[:, 8:16].reshape(rows, 512).astype(BF)
+            lanes = slice(g * 128, g * 128 + 128)
             for low in range(4):
                 cols = slice(low * 128, low * 128 + 128)
-                lm[low * rows : (low + 1) * rows, g * 128 : g * 128 + 128] = left[:, cols]
-                raw[low * rows : (low + 1) * rows, g * 128 : g * 128 + 128] = right[:, cols]
-        ordered = dot(order[...], raw[...]).astype(BF)
-        whole[block, core] = ordered.reshape(tiles // 2, 64, depth)
-        mine = whole.at[block, core]
-        pltpu.make_async_remote_copy(
-            mine, mine, sib_send.at[block, kind], sib_recv.at[block, kind],
-            device_id=sibling, device_id_type=MESH,
-        ).start()
+                lm[low * rows : (low + 1) * rows, lanes] = left[:, cols]
+                raw[low * rows : (low + 1) * rows, lanes] = right[:, cols]
+            ordered = dot(order[...], raw[:, lanes]).astype(BF)
+            whole[block, core, :, :, lanes] = ordered.reshape(tiles // 2, 64, 128)
+            mine = whole.at[block, core, :, :, lanes]
+            pltpu.make_async_remote_copy(
+                mine, mine, sib_send.at[block, kind], sib_recv.at[block, kind],
+                device_id=sibling, device_id_type=MESH,
+            ).start()
+
+    def triangle_out(block, kind):
+        rbuf, lm, raw, whole, ts, tr, order, groups, tiles = parts_of(kind)
+        rows = tiles * 8
+        full = kind == FULL
         other = whole.at[block, 1 - core]
         pltpu.make_async_copy(other, other, sib_recv.at[block, kind]).wait()
-        for g in range(groups):
-            right = jnp.concatenate(
-                [whole[block, 0, g], whole[block, 1, g]], axis=0
-            )
+        home = lax.bitwise_and(lax.shift_right_logical(gc, 2), groups - 1)
+        source = sy if full else sec * 2 + y
+
+        for turn in range(groups):
+            g = lax.bitwise_and(home + turn, groups - 1)
+            right = jnp.concatenate([whole[block, 0, g], whole[block, 1, g]], axis=0)
             product = dot_nt(lm[...], right).astype(BF)
             total = None
             for low in range(4):
@@ -219,51 +279,37 @@
                     tiles, 8, 128
                 )
 
-    def send_back(block, kind):
-        if kind == FULL:
-
             def send(step, carry):
-                to_gc, to_sy, device = place(step)
-                pltpu.make_async_remote_copy(
-                    ts_full.at[block, to_gc, to_sy], tr_full.at[block, me],
-                    back_send.at[block, kind], back_recv.at[block, kind],
-                    device_id=device, device_id_type=MESH,
-                ).start()
-                return carry
-
-            lax.fori_loop(1, 128, send, 0)
-            pltpu.make_async_copy(
-                ts_full.at[block, gc, sy], tr_full.at[block, me], back_recv.at[block, kind]
-            ).start()
-        else:
-
-            def send(step, carry):
-                to_gc = lax.bitwise_and(gc + step, 7)
-                to_q = lax.bitwise_and(sec * 2 + y + lax.shift_right_logical(step, 3), 3)
-                to_sec, to_y = lax.shift_right_logical(to_q, 1), lax.bitwise_and(to_q, 1)
-                itself = jnp.logical_and(
-                    to_gc == gc, jnp.logical_and(to_sec == sec, to_y == y)
-                )
-
-                @pl.when(itself)
-                def _():
+                to_gc = g * 4 + lax.bitwise_and(gc + step, 3)
+                to_tile = lax.bitwise_and(source + lax.shift_right_logical(step, 2), tiles - 1)
+                to_sec = lax.shift_right_logical(to_tile, 2 if full else 1)
+                to_y = lax.bitwise_and(to_tile, tiles // 2 - 1)
+
+                def local():
                     pltpu.make_async_copy(
-                        ts_half.at[block, to_gc, to_q], tr_half.at[block, me],
+                        ts.at[block, to_gc, to_tile], tr.at[block, channel],
                         back_recv.at[block, kind],
                     ).start()
 
-                @pl.when(jnp.logical_not(itself))
-                def _():
+                def remote():
                     pltpu.make_async_remote_copy(
-                        ts_half.at[block, to_gc, to_q], tr_half.at[block, me],
+                        ts.at[block, to_gc, to_tile], tr.at[block, channel],
                         back_send.at[block, kind], back_recv.at[block, kind],
                         device_id={"section": to_sec, "gr": to_y * 2 + core, "gc": to_gc},
                         device_id_type=MESH,
                     ).start()
 
+                if turn == 0:
+                    itself = step == 0
+                    if not full:
+                        itself = jnp.logical_and(itself, active)
+                    pl.when(itself)(local)
+                    pl.when(jnp.logical_not(itself))(remote)
+                else:
+                    remote()
                 return carry
 
-            lax.fori_loop(0, 32, send, 0)
+            lax.fori_loop(0, tiles * 4, send, 0)
 
     def finish(block, kind):
         z = zin if block == 0 else zout.at[0]
@@ -288,21 +334,20 @@
         stage[0:1024, :] = center.reshape(1024, 128)
         for r in range(8):
             tile = stage[pl.ds(r, 128, stride=8), :]
-            settled[r * 128 : r * 128 + 128] = tile.T.astype(BF)
+            settled[r * 128 : r * 128 + 128] = tile.astype(BF).T
         for part in range(4):
             rows = pl.ds(part * 256, 256)
             gate = sigmoid(dot(normed[kind, rows], w_gate[block]))
             update = dot(settled[rows], w_out[block])
             updated = (z[kind, rows].astype(F32) + gate * update).astype(BF)
-            updated = updated.astype(F32)
-            trans_in = norm_lanes(updated).astype(BF)
+            trans_in = norm_pair(updated, mean_of)
             gates = dot(trans_in, w_pin[block, :, 0:512])
             ups = dot(trans_in, w_pin[block, :, 512:1024])
-            inner = (gates * sigmoid(gates) * ups).astype(BF)
-            done = (updated + dot(inner, w_pout[block])).astype(BF)
+            inner = silu_times(gates, ups)
+            done = (updated.astype(F32) + dot(inner, w_pout[block])).astype(BF)
             zout[block, kind, rows] = done
             if block == 0:
-                normed[kind, rows] = norm_lanes(done.astype(F32)).astype(BF)
+                normed[kind, rows] = norm_pair(done, mean_of)
             else:
                 deliver(block, kind, part, 1)
 
@@ -329,7 +374,7 @@
             cols = part * 256
             gates = dot(value_in, st_in_v[:, cols : cols + 256])
             ups = dot(value_in, st_in_v[:, 1536 + cols : 1536 + cols + 256])
-            inner = (gates * sigmoid(gates) * ups).astype(BF)
+            inner = silu_times(gates, ups)
             total = total + dot(inner, st_out_v[cols : cols + 256])
         sout[...] = total.astype(BF)
 
@@ -362,38 +407,37 @@
                 single(sin_next)
 
     start_block(0)
+    forward(0, HALF)
     forward(0, FULL)
     more_weights()
-    forward(0, HALF)
     single_turn(0)
-    triangle(0, FULL)
-    send_back(0, FULL)
-    triangle(0, HALF)
-    send_back(0, HALF)
+    triangle_in(0, HALF)
+    triangle_out(0, HALF)
+    triangle_in(0, FULL)
+    triangle_out(0, FULL)
     rest_weights(0)
+    finish(0, HALF)
+    start_block(1)
+    forward(1, HALF)
     finish(0, FULL)
-    start_block(1)
     forward(1, FULL)
+    deliver(0, HALF)
     deliver(0, FULL)
-    finish(0, HALF)
-    forward(1, HALF)
-    deliver(0, HALF)
     single_turn(1)
-    triangle(1, FULL)
-    send_back(1, FULL)
-    triangle(1, HALF)
-    send_back(1, HALF)
+    triangle_in(1, HALF)
+    triangle_out(1, HALF)
+    triangle_in(1, FULL)
+    triangle_out(1, FULL)
     rest_weights(1)
+    finish(1, HALF)
     finish(1, FULL)
-    finish(1, HALF)
 
     def end_forward(block, kind):
-        sent = rbuf_full.at[block, pl.ds(0, 127)]
-        copy = pltpu.make_async_copy(sent, sent, fwd_send.at[block, kind])
-        if kind == FULL:
-            copy.wait()
-        else:
-            pl.when(active)(copy.wait)
+        sent = rbuf_full.at[block, pl.ds(0, 127 if kind == FULL else 28)]
+        pltpu.make_async_copy(sent, sent, fwd_send.at[block, kind]).wait()
+        if kind == HALF:
+            sent = sbuf.at[block, HALF, pl.ds(0, 120)]
+            pl.when(active)(pltpu.make_async_copy(sent, sent, relay_send.at[block]).wait)
 
     def end_triangle(block, kind):
         mine = (all_full if kind == FULL else all_half).at[block, core]
@@ -474,6 +518,9 @@
             pltpu.VMEM((2, 8, 4, 8, 128), BF),
             pltpu.VMEM((2, 128, 8, 128), BF),
             pltpu.VMEM((2, 128, 8, 128), BF),
+            pltpu.VMEM((2, 4, 8, 16, 128), BF),
+            dma((2,)),
+            dma((2,)),
             dma((2, 2)),
             dma((2, 2)),
             dma((2, 2)),
@@ -496,6 +543,7 @@
 
 
 def restore_kernel(lengths, staged, staged_single, out, sout, sems):
+    mean_of = jnp.full((128, 128), 1 / 128, BF)
     first = jnp.where(lengths[0] > lengths[1], 0, 1)
     copies = [
         pltpu.make_async_copy(staged.at[micro ^ first, half], out.at[0, micro, half], sems.at[micro, half])
@@ -518,7 +566,7 @@
             jax.ShapeDtypeStruct((128, 384), BF),
         ),
         in_specs=[pl.BlockSpec(memory_space=pltpu.SMEM), anywhere, anywhere],
-        out_specs=(anywhere, anywhere),
+        out_specs=(pl.BlockSpec(memory_space=pltpu.VMEM),) * 2,
         scratch_shapes=[pltpu.SemaphoreType.DMA((3, 2))],
     )(lengths, staged, staged_single)
 

time: 137 us -> 106 us (0.77)
  Pallas kernels: 135 us -> 105 us
    pallas_call x1, Pallas kernels: 36.6 us -> 2.91 us  [restore(): pl.pallas_call(restore_kernel, out_shape=(jax.ShapeDtypeStruct((1, 2, 2,...]
    pallas_call x1, Pallas kernels: 98.9 us -> 102 us  [trunk(): pl.pallas_call(trunk_kernel, out_shape=(jax.ShapeDtypeStruct((2, 2, 1024,...]
where the time goes in v2:
time: 106 us
  Pallas kernels  105 us (99%)
    pallas_call x1, Pallas kernels, trunk(): pl.pallas_call(trunk_kernel, out_shape=(jax.ShapeDtypeStruct((2, 2, 1024,...  102 us
    pallas_call x1, Pallas kernels, restore(): pl.pallas_call(restore_kernel, out_shape=(jax.ShapeDtypeStruct((1, 2, 2,...  2.91 us

profile of v2, /device:TPU:2, one launch (start us, length us, event | category | flops | bytes accessed | tf_op | source)
XLA Modules:
  0.0 106.1 jit_solution(5425937362729761697)
XLA Ops:
  0.6 102.4 %shard_map.113 = (bf16[2,2,1024,128]{3,2,1,0:T(8,128)(2,1)}, bf16[128,384]{1,0:T(8,128)(2,1)}) custom-call(s32[2]{0:T(128)} %lengths.3, bf16[2,64,32,128]{3,2,1,0:T(8,128)(2,1)} %pair.1, bf16[128,384]{1,0:T(8,128)(2,1)} %bitcast.15, bf16[128,512]{1,0:T(8,128)(2,1)} %bitcast.13, bf16[128,128]{1,0:T(8,128)(2,1)} %bitcast.16, bf16[128,128]{1,0:T(8,128)(2,1)} %bitcast.17, ...), custom_call_target="tpu_custom_call" | custom-call | tf_op jit(solution)/shard_map/pallas_call | solution.py:482
  103.0 2.9 %shard_map.114 = (bf16[1,2,2,1024,128]{4,3,2,1,0:T(8,128)(2,1)}, bf16[128,384]{1,0:T(8,128)(2,1)}) custom-call(s32[2]{0:T(128)} %lengths.3, bf16[2,2,1024,128]{3,2,1,0:T(8,128)(2,1)} %get-tuple-element.6.staged, bf16[128,384]{1,0:T(8,128)(2,1)} %get-tuple-element.7.staged_single), custom_call_target="tpu_custom_call" | custom-call | tf_op jit(solution)/shard_map/pallas_call | solution.py:562

commit v3 on v2

--- a/solution.py
+++ b/solution.py
@@ -7,6 +7,7 @@
 
 MESH = pl.DeviceIdType.MESH
 FULL, HALF = 0, 1
+RIGHT, LEFT = 0, 1
 BF = jnp.bfloat16
 F32 = jnp.float32
 
@@ -48,11 +49,11 @@
     lengths, pair, sin, tin, tgate, tout, pin, pout, st_in, st_out,
     out, sout,
     w_tin, w_gate, w_out, w_pin, w_pout, w_t, st_in_v, st_out_v, sin_next,
-    zin, zout, normed, stage, settled, perm, order_full, order_half,
-    sbuf, rbuf_full, rbuf_half, lm_full, raw_full, all_full, lm_half, raw_half, all_half,
+    own_sem, out_local, pair_in, zin, zout, normed, stage, settled, perm, order_full, order_half,
+    sfull, sbuf, rbuf_full, rbuf_half, lm_full, raw_full, all_full, lm_half, raw_half, all_half,
     ts_full, ts_half, tr_full, tr_half,
-    relayed, relay_send, relay_recv, fwd_send, fwd_recv, sib_send, sib_recv, back_send, back_recv,
-    met, w_send, w_recv, st_sem, single_send, single_recv, out_send, out_recv,
+    relayed, relay_send, relay_recv, full_send, full_recv, fwd_send, fwd_recv, sib_send, sib_recv, back_send, back_recv,
+    met, w_first, w_send, w_recv, st_sem, single_send, single_recv, out_send, out_recv,
 ):
     sec, gr, gc = lax.axis_index("section"), lax.axis_index("gr"), lax.axis_index("gc")
     y, core = lax.shift_right_logical(gr, 1), lax.bitwise_and(gr, 1)
@@ -80,7 +81,13 @@
         pltpu.make_async_copy(st_in, st_in_v, st_sem.at[0]),
         pltpu.make_async_copy(st_out, st_out_v, st_sem.at[1]),
     ]
-    for copy in st_copies:
+    weights = [(tin, w_tin), (tgate, w_gate), (tout, w_out), (pin, w_pin), (pout, w_pout)]
+    pair_copy = pltpu.make_async_copy(pair.at[:, pl.ds(sec * 32, 32)], pair_in, own_sem.at[5])
+    own_copies = [
+        pltpu.make_async_copy(own, held.at[sec], own_sem.at[index])
+        for index, (own, held) in enumerate(weights)
+    ]
+    for copy in [pair_copy] + own_copies + st_copies:
         copy.start()
 
     barrier = pltpu.get_barrier_semaphore()
@@ -103,10 +110,6 @@
         )
     greet_line(barrier)
 
-    weights = [(tin, w_tin), (tgate, w_gate), (tout, w_out), (pin, w_pin), (pout, w_pout)]
-    for own, held in weights:
-        held[sec] = own[...]
-
     def weight_copy(index):
         own, held = weights[index]
         return pltpu.make_async_remote_copy(
@@ -114,8 +117,16 @@
             device_id=peer, device_id_type=MESH,
         )
 
+    def first_copy(side):
+        cols = pl.ds(256 - 256 * side, 256)
+        return pltpu.make_async_remote_copy(
+            tin.at[:, cols], w_tin.at[sec, :, cols], w_first.at[0, side], w_first.at[1, side],
+            device_id=peer, device_id_type=MESH,
+        )
+
     pl.semaphore_wait(barrier, 23)
-    weight_copy(0).start()
+    first_copy(RIGHT).start()
+    first_copy(LEFT).start()
     greet_line(met)
 
     from_lane, to_lane = iota((128, 512), 0), iota((128, 512), 1)
@@ -129,12 +140,14 @@
     source = (o & 3) * 32 + ((o >> 5) & 1) * 16 + (o >> 6) * 8 + ((o >> 2) & 7)
     order_half[...] = jnp.where(i == source, 1.0, 0.0).astype(BF)
 
+    for copy in [pair_copy] + own_copies:
+        copy.wait()
     mean_of = jnp.full((128, 128), 1 / 128, BF)
     first = jnp.where(lengths[0] > lengths[1], 0, 1)
     for kind, crop in ((FULL, first), (HALF, 1 - first)):
         for part in range(4):
             rows = pl.ds(part * 256, 256)
-            z = pair[crop, pl.ds(sec * 32 + part * 8, 8)].reshape(256, 128)
+            z = pair_in[crop, part * 8 : part * 8 + 8].reshape(256, 128)
             zin[kind, rows] = z
             normed[kind, rows] = norm_pair(z, mean_of)
 
@@ -146,36 +159,47 @@
             held = weights[index][1].at[block]
             pltpu.make_async_copy(held, held, w_recv.at[index]).wait()
 
-    def project(block, kind):
+    def gated(block, side, values):
+        cols = slice(256 - 256 * side, 512 - 256 * side)
+        p = dot_nt(w_t[block, cols], values)
+        return sigmoid(p[0:128]) * p[128:256]
+
+    def project_full(block, side):
         for part in range(4):
-            rows = pl.ds(part * 256, 256)
-            p = dot_nt(w_t[...], normed[kind, rows])
-            left = sigmoid(p[0:128]) * p[128:256]
-            right = sigmoid(p[256:384]) * p[384:512]
+            value = gated(block, side, normed[FULL, pl.ds(part * 256, 256)])
             for sub in range(2):
-                cols = slice(sub * 128, sub * 128 + 128)
-                stage[pl.ds(part * 2 + sub, 128, stride=16), :] = left[:, cols]
-                stage[pl.ds(8 + part * 2 + sub, 128, stride=16), :] = right[:, cols]
+                stage[pl.ds(part * 2 + sub, 128, stride=8), :] = value[:, sub * 128 : sub * 128 + 128]
+        for part in range(4):
+            values = stage[part * 256 : part * 256 + 256, :].astype(BF)
+            sfull[block, side, part * 32 : part * 32 + 32] = values.reshape(32, 8, 128)
+
+    def project_half(block):
+        for part in range(4):
+            values = normed[HALF, pl.ds(part * 256, 256)]
+            for side in (LEFT, RIGHT):
+                value = gated(block, side, values)
+                row = part * 2 + 8 * (1 - side)
+                for sub in range(2):
+                    stage[pl.ds(row + sub, 128, stride=16), :] = value[:, sub * 128 : sub * 128 + 128]
         for part in range(8):
             values = stage[part * 256 : part * 256 + 256, :].astype(BF)
-            sbuf[block, kind, part * 16 : part * 16 + 16] = values.reshape(16, 16, 128)
-
-    def send_full(block, begin, end):
+            sbuf[block, part * 16 : part * 16 + 16] = values.reshape(16, 16, 128)
+
+    def send_full(block, side):
         def send(step, carry):
             to_gc, to_sy, device = place(step)
             pltpu.make_async_remote_copy(
-                sbuf.at[block, FULL, channel_of(to_gc, to_sy)], rbuf_full.at[block, slot],
-                fwd_send.at[block, FULL], fwd_recv.at[block, FULL],
+                sfull.at[block, side, channel_of(to_gc, to_sy)], rbuf_full.at[block, side, slot],
+                full_send.at[block, side], full_recv.at[block, side],
                 device_id=device, device_id_type=MESH,
             ).start()
             return carry
 
-        lax.fori_loop(begin, end, send, 0)
-        if begin == 1:
-            pltpu.make_async_copy(
-                sbuf.at[block, FULL, channel], rbuf_full.at[block, slot],
-                fwd_recv.at[block, FULL],
-            ).start()
+        lax.fori_loop(1, 128, send, 0)
+        pltpu.make_async_copy(
+            sfull.at[block, side, channel], rbuf_full.at[block, side, slot],
+            full_recv.at[block, side],
+        ).start()
 
     def send_half(block):
         source = sec * 2 + y
@@ -183,7 +207,7 @@
             to_plane = lax.bitwise_and(plane + step, 15)
             to_sy = lax.bitwise_and(to_plane, 7)
             pltpu.make_async_remote_copy(
-                sbuf.at[block, HALF, pl.ds(to_plane * 8, 8)], relayed.at[block, source],
+                sbuf.at[block, pl.ds(to_plane * 8, 8)], relayed.at[block, source],
                 relay_send.at[block], relay_recv.at[block],
                 device_id={
                     "section": lax.shift_right_logical(to_sy, 2),
@@ -193,7 +217,7 @@
                 device_id_type=MESH,
             ).start()
         pltpu.make_async_copy(
-            sbuf.at[block, HALF, pl.ds(plane * 8, 8)], relayed.at[block, source],
+            sbuf.at[block, pl.ds(plane * 8, 8)], relayed.at[block, source],
             relay_recv.at[block],
         ).start()
 
@@ -204,23 +228,22 @@
         for step in range(1, 8):
             to_z = lax.bitwise_and(z_at + step, 7)
             pltpu.make_async_remote_copy(
-                relayed.at[block, :, to_z], at, fwd_send.at[block, HALF], fwd_recv.at[block, HALF],
+                relayed.at[block, :, to_z], at, fwd_send.at[block], fwd_recv.at[block],
                 device_id={"section": sec, "gr": gr, "gc": x_hi * 8 + to_z},
                 device_id_type=MESH,
             ).start()
-        pltpu.make_async_copy(relayed.at[block, :, z_at], at, fwd_recv.at[block, HALF]).start()
+        pltpu.make_async_copy(relayed.at[block, :, z_at], at, fwd_recv.at[block]).start()
 
     def forward(block, kind):
         if kind == FULL:
-            project(block, FULL)
-            send_full(block, 1, 64)
-            relay(block)
-            send_full(block, 64, 128)
+            for side in (RIGHT, LEFT):
+                project_full(block, side)
+                send_full(block, side)
         else:
 
             @pl.when(active)
             def _():
-                project(block, HALF)
+                project_half(block)
                 send_half(block)
 
     def parts_of(kind):
@@ -228,33 +251,53 @@
             return rbuf_full, lm_full, raw_full, all_full, ts_full, tr_full, order_full, 4, 8
         return rbuf_half, lm_half, raw_half, all_half, ts_half, tr_half, order_half, 2, 4
 
-    def triangle_in(block, kind):
-        rbuf, lm, raw, whole, ts, tr, order, groups, tiles = parts_of(kind)
-        rows = tiles * 8
-        landed = rbuf.at[block]
-        pltpu.make_async_copy(landed, landed, fwd_recv.at[block, kind]).wait()
-        for g in range(groups):
+    def share_right(block, kind, g, ordered):
+        whole = all_full if kind == FULL else all_half
+        lanes = slice(g * 128, g * 128 + 128)
+        whole[block, core, :, :, lanes] = ordered.astype(BF).reshape(-1, 64, 128)
+        mine = whole.at[block, core, :, :, lanes]
+        pltpu.make_async_remote_copy(
+            mine, mine, sib_send.at[block, kind], sib_recv.at[block, kind],
+            device_id=sibling, device_id_type=MESH,
+        ).start()
+
+    def triangle_full(block, side):
+        landed = rbuf_full.at[block, side]
+        pltpu.make_async_copy(landed, landed, full_recv.at[block, side]).wait()
+        held = raw_full if side == RIGHT else lm_full
+        for g in range(4):
             total = None
             for low in range(4):
-                col = g * 4 + low
-                block_in = rbuf[block, col * tiles : (col + 1) * tiles].reshape(tiles * 16, 128)
+                col = (g * 4 + low) * 8
+                block_in = rbuf_full[block, side, col : col + 8].astype(F32)
+                term = dot(block_in.reshape(64, 128).astype(BF), perm[low])
+                total = term if total is None else total + term
+            total = total.astype(BF)
+            lanes = slice(g * 128, g * 128 + 128)
+            for low in range(4):
+                held[low * 64 : low * 64 + 64, lanes] = total[:, low * 128 : low * 128 + 128]
+            if side == RIGHT:
+                share_right(block, FULL, g, dot(order_full[...], raw_full[:, lanes]))
+
+    def triangle_half(block):
+        landed = rbuf_half.at[block]
+        pltpu.make_async_copy(landed, landed, fwd_recv.at[block]).wait()
+        for g in range(2):
+            total = None
+            for low in range(4):
+                col = (g * 4 + low) * 4
+                block_in = rbuf_half[block, col : col + 4].reshape(64, 128)
                 term = dot(block_in, perm[low])
                 total = term if total is None else total + term
-            total = total.reshape(tiles, 16, 512)
-            left = total[:, 0:8].reshape(rows, 512).astype(BF)
-            right = total[:, 8:16].reshape(rows, 512).astype(BF)
+            total = total.reshape(4, 16, 512)
+            left = total[:, 0:8].reshape(32, 512).astype(BF)
+            right = total[:, 8:16].reshape(32, 512).astype(BF)
             lanes = slice(g * 128, g * 128 + 128)
             for low in range(4):
                 cols = slice(low * 128, low * 128 + 128)
-                lm[low * rows : (low + 1) * rows, lanes] = left[:, cols]
-                raw[low * rows : (low + 1) * rows, lanes] = right[:, cols]
-            ordered = dot(order[...], raw[:, lanes]).astype(BF)
-            whole[block, core, :, :, lanes] = ordered.reshape(tiles // 2, 64, 128)
-            mine = whole.at[block, core, :, :, lanes]
-            pltpu.make_async_remote_copy(
-                mine, mine, sib_send.at[block, kind], sib_recv.at[block, kind],
-                device_id=sibling, device_id_type=MESH,
-            ).start()
+                lm_half[low * 32 : low * 32 + 32, lanes] = left[:, cols]
+                raw_half[low * 32 : low * 32 + 32, lanes] = right[:, cols]
+            share_right(block, HALF, g, dot(order_half[...], raw_half[:, lanes]))
 
     def triangle_out(block, kind):
         rbuf, lm, raw, whole, ts, tr, order, groups, tiles = parts_of(kind)
@@ -356,7 +399,9 @@
 
         @pl.when(sec == block)
         def _():
-            out[kind, sec, rows] = zout[block, kind, rows]
+            pltpu.make_async_copy(
+                zout.at[block, kind, rows], out.at[kind, sec, rows], out_local.at[kind]
+            ).start()
 
         @pl.when(sec != block)
         def _():
@@ -382,9 +427,15 @@
         sout, sin_next, single_send, single_recv, device_id=peer, device_id_type=MESH
     )
 
-    def start_block(block):
-        await_weight(block, 0)
-        w_t[...] = w_tin[block].astype(F32).T.astype(BF)
+    def start_block(block, side):
+        cols = slice(256 - 256 * side, 512 - 256 * side)
+
+        @pl.when(sec != block)
+        def _():
+            held = w_tin.at[block, :, cols]
+            pltpu.make_async_copy(held, held, w_first.at[1, side]).wait()
+
+        w_t[block, cols] = w_tin[block, :, cols].astype(F32).T.astype(BF)
 
     def more_weights():
         for index in range(1, 5):
@@ -406,37 +457,50 @@
                 single_copy.wait_recv()
                 single(sin_next)
 
-    start_block(0)
+    start_block(0, RIGHT)
+    project_full(0, RIGHT)
+    send_full(0, RIGHT)
+    start_block(0, LEFT)
+    project_full(0, LEFT)
+    send_full(0, LEFT)
     forward(0, HALF)
-    forward(0, FULL)
     more_weights()
     single_turn(0)
-    triangle_in(0, HALF)
+    triangle_full(0, RIGHT)
+    triangle_full(0, LEFT)
+    relay(0)
+    triangle_out(0, FULL)
+    triangle_half(0)
     triangle_out(0, HALF)
-    triangle_in(0, FULL)
-    triangle_out(0, FULL)
+    start_block(1, RIGHT)
+    start_block(1, LEFT)
     rest_weights(0)
-    finish(0, HALF)
-    start_block(1)
-    forward(1, HALF)
     finish(0, FULL)
     forward(1, FULL)
+    finish(0, HALF)
+    forward(1, HALF)
+    deliver(0, FULL)
     deliver(0, HALF)
-    deliver(0, FULL)
     single_turn(1)
-    triangle_in(1, HALF)
+    triangle_full(1, RIGHT)
+    triangle_full(1, LEFT)
+    relay(1)
+    triangle_out(1, FULL)
+    triangle_half(1)
     triangle_out(1, HALF)
-    triangle_in(1, FULL)
-    triangle_out(1, FULL)
     rest_weights(1)
+    finish(1, FULL)
     finish(1, HALF)
-    finish(1, FULL)
 
     def end_forward(block, kind):
-        sent = rbuf_full.at[block, pl.ds(0, 127 if kind == FULL else 28)]
-        pltpu.make_async_copy(sent, sent, fwd_send.at[block, kind]).wait()
-        if kind == HALF:
-            sent = sbuf.at[block, HALF, pl.ds(0, 120)]
+        if kind == FULL:
+            for side in (RIGHT, LEFT):
+                sent = rbuf_full.at[block, side, pl.ds(0, 127)]
+                pltpu.make_async_copy(sent, sent, full_send.at[block, side]).wait()
+        else:
+            sent = sbuf.at[block, pl.ds(0, 28)]
+            pltpu.make_async_copy(sent, sent, fwd_send.at[block]).wait()
+            sent = sbuf.at[block, pl.ds(0, 120)]
             pl.when(active)(pltpu.make_async_copy(sent, sent, relay_send.at[block]).wait)
 
     def end_triangle(block, kind):
@@ -455,13 +519,17 @@
             pl.when(jnp.logical_not(active))(lambda: wait(32))
 
     def end_rest():
-        for index in range(5):
+        first_copy(RIGHT).wait_send()
+        first_copy(LEFT).wait_send()
+        for index in range(1, 5):
             weight_copy(index).wait_send()
         pl.when(sec == 0)(single_copy.wait_send)
 
     def end_deliver(kind):
         given = zout.at[0, kind]
         pltpu.make_async_copy(given, given, out_send.at[kind]).wait()
+        kept = out.at[kind, sec]
+        pltpu.make_async_copy(kept, kept, out_local.at[kind]).wait()
         taken = out.at[kind, 1 - sec]
         pltpu.make_async_copy(taken, taken, out_recv.at[kind]).wait()
 
@@ -485,18 +553,21 @@
             jax.ShapeDtypeStruct((2, 2, 1024, 128), BF),
             jax.ShapeDtypeStruct((128, 384), BF),
         ),
-        in_specs=[pl.BlockSpec(memory_space=pltpu.SMEM)] + [vmem] * 7 + [anywhere] * 2,
-        out_specs=(vmem, vmem),
+        in_specs=[pl.BlockSpec(memory_space=pltpu.SMEM), anywhere, vmem] + [anywhere] * 7,
+        out_specs=(anywhere, vmem),
         scratch_shapes=[
             pltpu.VMEM((2, 128, 512), BF),
             pltpu.VMEM((2, 128, 128), BF),
             pltpu.VMEM((2, 128, 128), BF),
             pltpu.VMEM((2, 128, 1024), BF),
             pltpu.VMEM((2, 512, 128), BF),
-            pltpu.VMEM((512, 128), BF),
+            pltpu.VMEM((2, 512, 128), BF),
             pltpu.VMEM((384, 3072), BF),
             pltpu.VMEM((1536, 384), BF),
             pltpu.VMEM((128, 384), BF),
+            dma((6,)),
+            dma((2,)),
+            pltpu.VMEM((2, 32, 32, 128), BF),
             pltpu.VMEM((2, 1024, 128), BF),
             pltpu.VMEM((2, 2, 1024, 128), BF),
             pltpu.VMEM((2, 1024, 128), BF),
@@ -505,8 +576,9 @@
             pltpu.VMEM((4, 128, 512), BF),
             pltpu.VMEM((256, 256), BF),
             pltpu.VMEM((128, 128), BF),
-            pltpu.VMEM((2, 2, 128, 16, 128), BF),
+            pltpu.VMEM((2, 2, 128, 8, 128), BF),
             pltpu.VMEM((2, 128, 16, 128), BF),
+            pltpu.VMEM((2, 2, 128, 8, 128), BF),
             pltpu.VMEM((2, 32, 16, 128), BF),
             pltpu.VMEM((256, 512), BF),
             pltpu.VMEM((256, 512), BF),
@@ -523,11 +595,14 @@
             dma((2,)),
             dma((2, 2)),
             dma((2, 2)),
+            dma((2,)),
+            dma((2,)),
             dma((2, 2)),
             dma((2, 2)),
             dma((2, 2)),
             dma((2, 2)),
             pltpu.SemaphoreType.REGULAR,
+            dma((2, 2)),
             dma((5,)),
             dma((5,)),
             dma((2,)),
@@ -543,7 +618,6 @@
 
 
 def restore_kernel(lengths, staged, staged_single, out, sout, sems):
-    mean_of = jnp.full((128, 128), 1 / 128, BF)
     first = jnp.where(lengths[0] > lengths[1], 0, 1)
     copies = [
         pltpu.make_async_copy(staged.at[micro ^ first, half], out.at[0, micro, half], sems.at[micro, half])

time: 106 us -> 99.9 us (0.942)
  Pallas kernels: 105 us -> 99 us
    pallas_call x1, Pallas kernels: 102 us -> 96 us  [trunk(): pl.pallas_call(trunk_kernel, out_shape=(jax.ShapeDtypeStruct((2, 2, 1024,...]
where the time goes in v3:
time: 99.9 us; the launch traced here: 99.8 us
  Pallas kernels  99 us (99%)
    pallas_call x1, Pallas kernels, trunk(): pl.pallas_call(trunk_kernel, out_shape=(jax.ShapeDtypeStruct((2, 2, 1024,...  96 us
    pallas_call x1, Pallas kernels, restore(): pl.pallas_call(restore_kernel, out_shape=(jax.ShapeDtypeStruct((1, 2, 2,...  2.91 us

profile of v3, /device:TPU:2, one launch (start us, length us, event | category | flops | bytes accessed | tf_op | source)
XLA Modules:
  0.0 99.8 jit_solution(13192706640299346216)
XLA Ops:
  0.6 96.0 %shard_map.113 = (bf16[2,2,1024,128]{3,2,1,0:T(8,128)(2,1)}, bf16[128,384]{1,0:T(8,128)(2,1)}) custom-call(s32[2]{0:T(128)} %lengths.3, bf16[2,64,32,128]{3,2,1,0:T(8,128)(2,1)} %pair.1, bf16[128,384]{1,0:T(8,128)(2,1)} %bitcast.15, bf16[128,512]{1,0:T(8,128)(2,1)} %bitcast.13, bf16[128,128]{1,0:T(8,128)(2,1)} %bitcast.16, bf16[128,128]{1,0:T(8,128)(2,1)} %bitcast.17, ...), custom_call_target="tpu_custom_call" | custom-call | tf_op jit(solution)/shard_map/pallas_call | solution.py:550
  96.7 2.9 %shard_map.114 = (bf16[1,2,2,1024,128]{4,3,2,1,0:T(8,128)(2,1)}, bf16[128,384]{1,0:T(8,128)(2,1)}) custom-call(s32[2]{0:T(128)} %lengths.3, bf16[2,2,1024,128]{3,2,1,0:T(8,128)(2,1)} %get-tuple-element.6.staged, bf16[128,384]{1,0:T(8,128)(2,1)} %get-tuple-element.7.staged_single), custom_call_target="tpu_custom_call" | custom-call | tf_op jit(solution)/shard_map/pallas_call | solution.py:636

commit v4 on v3

--- a/solution.py
+++ b/solution.py
@@ -28,12 +28,6 @@
     center = v - jnp.mean(v, axis=-1, keepdims=True)
     spread = jnp.mean(center * center, axis=-1, keepdims=True)
     return center * lax.rsqrt(spread + 1e-05)
-
-
-def norm_pair(v, mean_of):
-    center = v.astype(F32) - dot(v, mean_of)
-    spread = dot((center * center).astype(BF), mean_of)
-    return (center * lax.rsqrt(spread + 1e-05)).astype(BF)
 
 
 def silu_times(gates, ups):
@@ -142,14 +136,11 @@
 
     for copy in [pair_copy] + own_copies:
         copy.wait()
-    mean_of = jnp.full((128, 128), 1 / 128, BF)
     first = jnp.where(lengths[0] > lengths[1], 0, 1)
     for kind, crop in ((FULL, first), (HALF, 1 - first)):
-        for part in range(4):
-            rows = pl.ds(part * 256, 256)
-            z = pair_in[crop, part * 8 : part * 8 + 8].reshape(256, 128)
-            zin[kind, rows] = z
-            normed[kind, rows] = norm_pair(z, mean_of)
+        z = pair_in[crop].reshape(1024, 128)
+        zin[kind] = z
+        normed[kind] = norm_lanes(z.astype(F32)).astype(BF)
 
     pl.semaphore_wait(met, 15)
 
@@ -165,10 +156,10 @@
         return sigmoid(p[0:128]) * p[128:256]
 
     def project_full(block, side):
-        for part in range(4):
-            value = gated(block, side, normed[FULL, pl.ds(part * 256, 256)])
-            for sub in range(2):
-                stage[pl.ds(part * 2 + sub, 128, stride=8), :] = value[:, sub * 128 : sub * 128 + 128]
+        for part in range(2):
+            value = gated(block, side, normed[FULL, pl.ds(part * 512, 512)])
+            for sub in range(4):
+                stage[pl.ds(part * 4 + sub, 128, stride=8), :] = value[:, sub * 128 : sub * 128 + 128]
         for part in range(4):
             values = stage[part * 256 : part * 256 + 256, :].astype(BF)
             sfull[block, side, part * 32 : part * 32 + 32] = values.reshape(32, 8, 128)
@@ -378,24 +369,25 @@
         for r in range(8):
             tile = stage[pl.ds(r, 128, stride=8), :]
             settled[r * 128 : r * 128 + 128] = tile.astype(BF).T
-        for part in range(4):
-            rows = pl.ds(part * 256, 256)
+        parts = 1 if block == 0 else 2
+        for part in range(parts):
+            rows = pl.ds(part * (1024 // parts), 1024 // parts)
             gate = sigmoid(dot(normed[kind, rows], w_gate[block]))
             update = dot(settled[rows], w_out[block])
             updated = (z[kind, rows].astype(F32) + gate * update).astype(BF)
-            trans_in = norm_pair(updated, mean_of)
+            trans_in = norm_lanes(updated.astype(F32)).astype(BF)
             gates = dot(trans_in, w_pin[block, :, 0:512])
             ups = dot(trans_in, w_pin[block, :, 512:1024])
             inner = silu_times(gates, ups)
             done = (updated.astype(F32) + dot(inner, w_pout[block])).astype(BF)
             zout[block, kind, rows] = done
             if block == 0:
-                normed[kind, rows] = norm_pair(done, mean_of)
+                normed[kind, rows] = norm_lanes(done.astype(F32)).astype(BF)
             else:
-                deliver(block, kind, part, 1)
-
-    def deliver(block, kind, part=0, parts=4):
-        rows = pl.ds(part * 256, parts * 256)
+                deliver(block, kind, part, parts)
+
+    def deliver(block, kind, part=0, parts=1):
+        rows = pl.ds(part * (1024 // parts), 1024 // parts)
 
         @pl.when(sec == block)
         def _():

time: 99.9 us -> 96.8 us (0.969)
  Pallas kernels: 99 us -> 95.9 us
    pallas_call x1, Pallas kernels: 96 us -> 93 us  [trunk(): pl.pallas_call(trunk_kernel, out_shape=(jax.ShapeDtypeStruct((2, 2, 1024,...]
where the time goes in v4:
time: 96.8 us; the launch traced here: 96.7 us
  Pallas kernels  95.9 us (99%)
    pallas_call x1, Pallas kernels, trunk(): pl.pallas_call(trunk_kernel, out_shape=(jax.ShapeDtypeStruct((2, 2, 1024,...  93 us
    pallas_call x1, Pallas kernels, restore(): pl.pallas_call(restore_kernel, out_shape=(jax.ShapeDtypeStruct((1, 2, 2,...  2.91 us

profile of v4, /device:TPU:2, one launch (start us, length us, event | category | flops | bytes accessed | tf_op | source)
XLA Modules:
  0.0 96.7 jit_solution(17176146555783166966)
XLA Ops:
  0.6 93.0 %shard_map.113 = (bf16[2,2,1024,128]{3,2,1,0:T(8,128)(2,1)}, bf16[128,384]{1,0:T(8,128)(2,1)}) custom-call(s32[2]{0:T(128)} %lengths.3, bf16[2,64,32,128]{3,2,1,0:T(8,128)(2,1)} %pair.1, bf16[128,384]{1,0:T(8,128)(2,1)} %bitcast.15, bf16[128,512]{1,0:T(8,128)(2,1)} %bitcast.13, bf16[128,128]{1,0:T(8,128)(2,1)} %bitcast.16, bf16[128,128]{1,0:T(8,128)(2,1)} %bitcast.17, ...), custom_call_target="tpu_custom_call" | custom-call | tf_op jit(solution)/shard_map/pallas_call | solution.py:542
  93.6 2.9 %shard_map.114 = (bf16[1,2,2,1024,128]{4,3,2,1,0:T(8,128)(2,1)}, bf16[128,384]{1,0:T(8,128)(2,1)}) custom-call(s32[2]{0:T(128)} %lengths.3, bf16[2,2,1024,128]{3,2,1,0:T(8,128)(2,1)} %get-tuple-element.6.staged, bf16[128,384]{1,0:T(8,128)(2,1)} %get-tuple-element.7.staged_single), custom_call_target="tpu_custom_call" | custom-call | tf_op jit(solution)/shard_map/pallas_call | solution.py:628

commit v5 on v4

--- a/solution.py
+++ b/solution.py
@@ -45,7 +45,7 @@
     w_tin, w_gate, w_out, w_pin, w_pout, w_t, st_in_v, st_out_v, sin_next,
     own_sem, out_local, pair_in, zin, zout, normed, stage, settled, perm, order_full, order_half,
     sfull, sbuf, rbuf_full, rbuf_half, lm_full, raw_full, all_full, lm_half, raw_half, all_half,
-    ts_full, ts_half, tr_full, tr_half,
+    ts_full, ts_half, tr_full, tr_half, tr_last, z_peer, normed_peer, zlast, peer_send, peer_recv,
     relayed, relay_send, relay_recv, full_send, full_recv, fwd_send, fwd_recv, sib_send, sib_recv, back_send, back_recv,
     met, w_first, w_send, w_recv, st_sem, single_send, single_recv, out_send, out_recv,
 ):
@@ -239,8 +239,8 @@
 
     def parts_of(kind):
         if kind == FULL:
-            return rbuf_full, lm_full, raw_full, all_full, ts_full, tr_full, order_full, 4, 8
-        return rbuf_half, lm_half, raw_half, all_half, ts_half, tr_half, order_half, 2, 4
+            return lm_full, all_full, ts_full, 4, 8
+        return lm_half, all_half, ts_half, 2, 4
 
     def share_right(block, kind, g, ordered):
         whole = all_full if kind == FULL else all_half
@@ -291,7 +291,7 @@
             share_right(block, HALF, g, dot(order_half[...], raw_half[:, lanes]))
 
     def triangle_out(block, kind):
-        rbuf, lm, raw, whole, ts, tr, order, groups, tiles = parts_of(kind)
+        lm, whole, ts, groups, tiles = parts_of(kind)
         rows = tiles * 8
         full = kind == FULL
         other = whole.at[block, 1 - core]
@@ -319,15 +319,23 @@
                 to_sec = lax.shift_right_logical(to_tile, 2 if full else 1)
                 to_y = lax.bitwise_and(to_tile, tiles // 2 - 1)
 
+                if full:
+                    target = tr_full.at[block, channel]
+                elif block == 0:
+                    target = tr_half.at[channel]
+                else:
+                    target = tr_last.at[to_sec, channel]
+                    to_sec = 1
+
                 def local():
                     pltpu.make_async_copy(
-                        ts.at[block, to_gc, to_tile], tr.at[block, channel],
+                        ts.at[block, to_gc, to_tile], target,
                         back_recv.at[block, kind],
                     ).start()
 
                 def remote():
                     pltpu.make_async_remote_copy(
-                        ts.at[block, to_gc, to_tile], tr.at[block, channel],
+                        ts.at[block, to_gc, to_tile], target,
                         back_send.at[block, kind], back_recv.at[block, kind],
                         device_id={"section": to_sec, "gr": to_y * 2 + core, "gc": to_gc},
                         device_id_type=MESH,
@@ -335,6 +343,9 @@
 
                 if turn == 0:
                     itself = step == 0
+                    if not full and block == 1:
+                        itself = jnp.logical_and(to_gc == gc, to_y == y)
+                        itself = jnp.logical_and(itself, sec == 1)
                     if not full:
                         itself = jnp.logical_and(itself, active)
                     pl.when(itself)(local)
@@ -345,23 +356,8 @@
 
             lax.fori_loop(0, tiles * 4, send, 0)
 
-    def finish(block, kind):
-        z = zin if block == 0 else zout.at[0]
-        tr = tr_full if kind == FULL else tr_half
-        landed = tr.at[block]
-        if kind == FULL:
-            pltpu.make_async_copy(landed, landed, back_recv.at[block, kind]).wait()
-        else:
-
-            @pl.when(active)
-            def _():
-                pltpu.make_async_copy(landed, landed, back_recv.at[block, kind]).wait()
-
-            @pl.when(jnp.logical_not(active))
-            def _():
-                tr[block] = jnp.zeros((128, 8, 128), BF)
-
-        values = tr[block].astype(F32)
+    def complete(block, tr, z, normed_in, parts, put):
+        values = tr[...].astype(F32)
         center = values - jnp.mean(values, axis=0, keepdims=True)
         spread = jnp.mean(center * center, axis=0, keepdims=True)
         center = center * lax.rsqrt(spread + 1e-05)
@@ -369,22 +365,71 @@
         for r in range(8):
             tile = stage[pl.ds(r, 128, stride=8), :]
             settled[r * 128 : r * 128 + 128] = tile.astype(BF).T
-        parts = 1 if block == 0 else 2
         for part in range(parts):
             rows = pl.ds(part * (1024 // parts), 1024 // parts)
-            gate = sigmoid(dot(normed[kind, rows], w_gate[block]))
+            gate = sigmoid(dot(normed_in[rows], w_gate[block]))
             update = dot(settled[rows], w_out[block])
-            updated = (z[kind, rows].astype(F32) + gate * update).astype(BF)
+            updated = (z[rows].astype(F32) + gate * update).astype(BF)
             trans_in = norm_lanes(updated.astype(F32)).astype(BF)
             gates = dot(trans_in, w_pin[block, :, 0:512])
             ups = dot(trans_in, w_pin[block, :, 512:1024])
             inner = silu_times(gates, ups)
             done = (updated.astype(F32) + dot(inner, w_pout[block])).astype(BF)
+            put(part, rows, done)
+
+    def await_back(block, kind, landed):
+        if kind == FULL:
+            pltpu.make_async_copy(landed, landed, back_recv.at[block, kind]).wait()
+        else:
+
+            @pl.when(active)
+            def _():
+                pltpu.make_async_copy(landed, landed, back_recv.at[block, kind]).wait()
+
+            @pl.when(jnp.logical_not(active))
+            def _():
+                landed[...] = jnp.zeros(landed.shape, BF)
+
+    def finish(block, kind):
+        z = (zin if block == 0 else zout.at[0]).at[kind]
+        landed = tr_full.at[block] if kind == FULL else tr_half
+        parts = 1 if block == 0 else 2
+        await_back(block, kind, landed)
+
+        def put(part, rows, done):
             zout[block, kind, rows] = done
             if block == 0:
                 normed[kind, rows] = norm_lanes(done.astype(F32)).astype(BF)
             else:
                 deliver(block, kind, part, parts)
+
+        complete(block, landed, z, normed.at[kind], parts, put)
+
+    def finish_last():
+        await_back(1, HALF, tr_last)
+        pltpu.make_async_copy(z_peer, z_peer, peer_recv).wait()
+        normed_peer[...] = norm_lanes(z_peer[...].astype(F32)).astype(BF)
+        for half in range(2):
+
+            def put(part, rows, done):
+                zlast[half, rows] = done
+                pltpu.make_async_copy(
+                    zlast.at[half, rows], out.at[HALF, half, rows], out_local.at[HALF]
+                ).start()
+
+            own = half == 1
+            complete(
+                1,
+                tr_last.at[half],
+                zout.at[0, HALF] if own else z_peer,
+                normed.at[HALF] if own else normed_peer,
+                1,
+                put,
+            )
+
+    peer_copy = pltpu.make_async_remote_copy(
+        zout.at[0, HALF], z_peer, peer_send, peer_recv, device_id=peer, device_id_type=MESH
+    )
 
     def deliver(block, kind, part=0, parts=1):
         rows = pl.ds(part * (1024 // parts), 1024 // parts)
@@ -473,6 +518,7 @@
     forward(1, HALF)
     deliver(0, FULL)
     deliver(0, HALF)
+    pl.when(sec == 0)(peer_copy.start)
     single_turn(1)
     triangle_full(1, RIGHT)
     triangle_full(1, LEFT)
@@ -481,8 +527,9 @@
     triangle_half(1)
     triangle_out(1, HALF)
     rest_weights(1)
+    pl.when(jnp.logical_and(sec == 1, jnp.logical_not(active)))(finish_last)
     finish(1, FULL)
-    finish(1, HALF)
+    pl.when(jnp.logical_and(sec == 1, active))(finish_last)
 
     def end_forward(block, kind):
         if kind == FULL:
@@ -507,8 +554,9 @@
         if kind == FULL:
             wait(127)
         else:
-            pl.when(active)(lambda: wait(31))
-            pl.when(jnp.logical_not(active))(lambda: wait(32))
+            own = active if block == 0 else jnp.logical_and(active, sec == 1)
+            pl.when(own)(lambda: wait(31 if block == 0 else 30))
+            pl.when(jnp.logical_not(own))(lambda: wait(32))
 
     def end_rest():
         first_copy(RIGHT).wait_send()
@@ -518,12 +566,28 @@
         pl.when(sec == 0)(single_copy.wait_send)
 
     def end_deliver(kind):
-        given = zout.at[0, kind]
-        pltpu.make_async_copy(given, given, out_send.at[kind]).wait()
+        given = pltpu.make_async_copy(zout.at[0, kind], zout.at[0, kind], out_send.at[kind])
         kept = out.at[kind, sec]
-        pltpu.make_async_copy(kept, kept, out_local.at[kind]).wait()
+        kept = pltpu.make_async_copy(kept, kept, out_local.at[kind])
         taken = out.at[kind, 1 - sec]
-        pltpu.make_async_copy(taken, taken, out_recv.at[kind]).wait()
+        taken = pltpu.make_async_copy(taken, taken, out_recv.at[kind])
+        if kind == FULL:
+            given.wait()
+            kept.wait()
+            taken.wait()
+        else:
+
+            @pl.when(sec == 0)
+            def _():
+                peer_copy.wait_send()
+                kept.wait()
+                taken.wait()
+
+            @pl.when(sec == 1)
+            def _():
+                given.wait()
+                both = out.at[kind]
+                pltpu.make_async_copy(both, both, out_local.at[kind]).wait()
 
     for block in range(2):
         for kind in (FULL, HALF):
@@ -581,7 +645,13 @@
             pltpu.VMEM((2, 16, 8, 8, 128), BF),
             pltpu.VMEM((2, 8, 4, 8, 128), BF),
             pltpu.VMEM((2, 128, 8, 128), BF),
+            pltpu.VMEM((128, 8, 128), BF),
             pltpu.VMEM((2, 128, 8, 128), BF),
+            pltpu.VMEM((1024, 128), BF),
+            pltpu.VMEM((1024, 128), BF),
+            pltpu.VMEM((2, 1024, 128), BF),
+            dma,
+            dma,
             pltpu.VMEM((2, 4, 8, 16, 128), BF),
             dma((2,)),
             dma((2,)),

time: 96.8 us -> 91.4 us (0.944)
  Pallas kernels: 95.9 us -> 90.2 us
    pallas_call x1, Pallas kernels: 93 us -> 87.3 us  [trunk(): pl.pallas_call(trunk_kernel, out_shape=(jax.ShapeDtypeStruct((2, 2, 1024,...]
where the time goes in v5:
time: 91.4 us; the launch traced here: 91 us
  Pallas kernels  90.2 us (99%)
    pallas_call x1, Pallas kernels, trunk(): pl.pallas_call(trunk_kernel, out_shape=(jax.ShapeDtypeStruct((2, 2, 1024,...  87.3 us
    pallas_call x1, Pallas kernels, restore(): pl.pallas_call(restore_kernel, out_shape=(jax.ShapeDtypeStruct((1, 2, 2,...  2.91 us

profile of v5, /device:TPU:2, one launch (start us, length us, event | category | flops | bytes accessed | tf_op | source)
XLA Modules:
  0.0 91.0 jit_solution(18320848155772908920)
XLA Ops:
  0.6 87.3 %shard_map.113 = (bf16[2,2,1024,128]{3,2,1,0:T(8,128)(2,1)}, bf16[128,384]{1,0:T(8,128)(2,1)}) custom-call(s32[2]{0:T(128)} %lengths.3, bf16[2,64,32,128]{3,2,1,0:T(8,128)(2,1)} %pair.1, bf16[128,384]{1,0:T(8,128)(2,1)} %bitcast.15, bf16[128,512]{1,0:T(8,128)(2,1)} %bitcast.13, bf16[128,128]{1,0:T(8,128)(2,1)} %bitcast.16, bf16[128,128]{1,0:T(8,128)(2,1)} %bitcast.17, ...), custom_call_target="tpu_custom_call" | custom-call | tf_op jit(solution)/shard_map/pallas_call | solution.py:606
  87.9 2.9 %shard_map.114 = (bf16[1,2,2,1024,128]{4,3,2,1,0:T(8,128)(2,1)}, bf16[128,384]{1,0:T(8,128)(2,1)}) custom-call(s32[2]{0:T(128)} %lengths.3, bf16[2,2,1024,128]{3,2,1,0:T(8,128)(2,1)} %get-tuple-element.6.staged, bf16[128,384]{1,0:T(8,128)(2,1)} %get-tuple-element.7.staged_single), custom_call_target="tpu_custom_call" | custom-call | tf_op jit(solution)/shard_map/pallas_call | solution.py:698

commit v6 on v5

--- a/solution.py
+++ b/solution.py
@@ -177,16 +177,24 @@
             sbuf[block, part * 16 : part * 16 + 16] = values.reshape(16, 16, 128)
 
     def send_full(block, side):
-        def send(step, carry):
-            to_gc, to_sy, device = place(step)
-            pltpu.make_async_remote_copy(
-                sfull.at[block, side, channel_of(to_gc, to_sy)], rbuf_full.at[block, side, slot],
-                full_send.at[block, side], full_recv.at[block, side],
-                device_id=device, device_id_type=MESH,
-            ).start()
-            return carry
-
-        lax.fori_loop(1, 128, send, 0)
+        for turn in range(8):
+            to_sy = lax.bitwise_and(sy + turn, 7)
+            to_row = lax.bitwise_and(to_sy, 3) * 2 + core
+            to_sec = lax.shift_right_logical(to_sy, 2)
+
+            def send(step, carry):
+                to_gc = lax.bitwise_and(gc + step, 15)
+                pltpu.make_async_remote_copy(
+                    sfull.at[block, side, channel_of(to_gc, to_sy)],
+                    rbuf_full.at[block, side, slot],
+                    full_send.at[block, side], full_recv.at[block, side],
+                    device_id={"section": to_sec, "gr": to_row, "gc": to_gc},
+                    device_id_type=MESH,
+                ).start()
+                return carry
+
+            first = 1 if turn == 0 else 0
+            lax.fori_loop(first, 16, send, 0, unroll=5 if turn == 0 else 4)
         pltpu.make_async_copy(
             sfull.at[block, side, channel], rbuf_full.at[block, side, slot],
             full_recv.at[block, side],
@@ -354,7 +362,7 @@
                     remote()
                 return carry
 
-            lax.fori_loop(0, tiles * 4, send, 0)
+            lax.fori_loop(0, tiles * 4, send, 0, unroll=4)
 
     def complete(block, tr, z, normed_in, parts, put):
         values = tr[...].astype(F32)
@@ -498,14 +506,14 @@
     project_full(0, RIGHT)
     send_full(0, RIGHT)
     start_block(0, LEFT)
+    forward(0, HALF)
     project_full(0, LEFT)
     send_full(0, LEFT)
-    forward(0, HALF)
     more_weights()
     single_turn(0)
     triangle_full(0, RIGHT)
+    relay(0)
     triangle_full(0, LEFT)
-    relay(0)
     triangle_out(0, FULL)
     triangle_half(0)
     triangle_out(0, HALF)
@@ -513,16 +521,19 @@
     start_block(1, LEFT)
     rest_weights(0)
     finish(0, FULL)
-    forward(1, FULL)
+    project_full(1, RIGHT)
+    send_full(1, RIGHT)
     finish(0, HALF)
     forward(1, HALF)
+    project_full(1, LEFT)
+    send_full(1, LEFT)
     deliver(0, FULL)
     deliver(0, HALF)
     pl.when(sec == 0)(peer_copy.start)
     single_turn(1)
     triangle_full(1, RIGHT)
+    relay(1)
     triangle_full(1, LEFT)
-    relay(1)
     triangle_out(1, FULL)
     triangle_half(1)
     triangle_out(1, HALF)

time: 91.4 us -> 88.2 us (0.965)
  Pallas kernels: 90.2 us -> 87.2 us
    pallas_call x1, Pallas kernels: 87.3 us -> 84.3 us  [trunk(): pl.pallas_call(trunk_kernel, out_shape=(jax.ShapeDtypeStruct((2, 2, 1024,...]
where the time goes in v6:
time: 88.2 us; the launch traced here: 88 us
  Pallas kernels  87.2 us (99%)
    pallas_call x1, Pallas kernels, trunk(): pl.pallas_call(trunk_kernel, out_shape=(jax.ShapeDtypeStruct((2, 2, 1024,...  84.3 us
    pallas_call x1, Pallas kernels, restore(): pl.pallas_call(restore_kernel, out_shape=(jax.ShapeDtypeStruct((1, 2, 2,...  2.91 us

profile of v6, /device:TPU:2, one launch (start us, length us, event | category | flops | bytes accessed | tf_op | source)
XLA Modules:
  0.0 88.0 jit_solution(13593752100801649427)
XLA Ops:
  0.6 84.3 %shard_map.113 = (bf16[2,2,1024,128]{3,2,1,0:T(8,128)(2,1)}, bf16[128,384]{1,0:T(8,128)(2,1)}) custom-call(s32[2]{0:T(128)} %lengths.3, bf16[2,64,32,128]{3,2,1,0:T(8,128)(2,1)} %pair.1, bf16[128,384]{1,0:T(8,128)(2,1)} %bitcast.15, bf16[128,512]{1,0:T(8,128)(2,1)} %bitcast.13, bf16[128,128]{1,0:T(8,128)(2,1)} %bitcast.16, bf16[128,128]{1,0:T(8,128)(2,1)} %bitcast.17, ...), custom_call_target="tpu_custom_call" | custom-call | tf_op jit(solution)/shard_map/pallas_call | solution.py:617
  84.9 2.9 %shard_map.114 = (bf16[1,2,2,1024,128]{4,3,2,1,0:T(8,128)(2,1)}, bf16[128,384]{1,0:T(8,128)(2,1)}) custom-call(s32[2]{0:T(128)} %lengths.3, bf16[2,2,1024,128]{3,2,1,0:T(8,128)(2,1)} %get-tuple-element.6.staged, bf16[128,384]{1,0:T(8,128)(2,1)} %get-tuple-element.7.staged_single), custom_call_target="tpu_custom_call" | custom-call | tf_op jit(solution)/shard_map/pallas_call | solution.py:709

commit v7 on v6

--- a/solution.py
+++ b/solution.py
@@ -690,17 +690,28 @@
     )(lengths, pair, sin, tin, tgate, tout, pin, pout, st_in, st_out)
 
 
-def restore_kernel(lengths, staged, staged_single, out, sout, sems):
+def restore_kernel(lengths, staged, staged_single, out, sout, held, held_single, arrive, leave):
     first = jnp.where(lengths[0] > lengths[1], 0, 1)
-    copies = [
-        pltpu.make_async_copy(staged.at[micro ^ first, half], out.at[0, micro, half], sems.at[micro, half])
+    steps = [
+        (staged.at[micro ^ first, half], held.at[micro, half], out.at[0, micro, half])
         for micro in range(2)
         for half in range(2)
     ]
-    copies.append(pltpu.make_async_copy(staged_single, sout, sems.at[2, 0]))
-    for copy in copies:
+    steps.append((staged_single, held_single, sout))
+    taken = [
+        pltpu.make_async_copy(source, kept, arrive.at[index])
+        for index, (source, kept, target) in enumerate(steps)
+    ]
+    given = [
+        pltpu.make_async_copy(kept, target, leave.at[index])
+        for index, (source, kept, target) in enumerate(steps)
+    ]
+    for copy in taken:
         copy.start()
-    for copy in copies:
+    for arrived, onward in zip(taken, given):
+        arrived.wait()
+        onward.start()
+    for copy in given:
         copy.wait()
 
 
@@ -713,8 +724,13 @@
             jax.ShapeDtypeStruct((128, 384), BF),
         ),
         in_specs=[pl.BlockSpec(memory_space=pltpu.SMEM), anywhere, anywhere],
-        out_specs=(pl.BlockSpec(memory_space=pltpu.VMEM),) * 2,
-        scratch_shapes=[pltpu.SemaphoreType.DMA((3, 2))],
+        out_specs=(anywhere, anywhere),
+        scratch_shapes=[
+            pltpu.VMEM((2, 2, 1024, 128), BF),
+            pltpu.VMEM((128, 384), BF),
+            pltpu.SemaphoreType.DMA((5,)),
+            pltpu.SemaphoreType.DMA((5,)),
+        ],
     )(lengths, staged, staged_single)
 
 

time: 88.2 us -> 88 us (level)
  no operation moved by 1% of the time
where the time goes in v7:
time: 88 us; the launch traced here: 87.7 us
  Pallas kernels  86.9 us (99%)
    pallas_call x1, Pallas kernels, trunk(): pl.pallas_call(trunk_kernel, out_shape=(jax.ShapeDtypeStruct((2, 2, 1024,...  84.3 us
    pallas_call x1, Pallas kernels, restore(): pl.pallas_call(restore_kernel, out_shape=(jax.ShapeDtypeStruct((1, 2, 2,...  2.69 us

profile of v7, /device:TPU:2, one launch (start us, length us, event | category | flops | bytes accessed | tf_op | source)
XLA Modules:
  0.0 87.7 jit_solution(7705586808080065646)
XLA Ops:
  0.6 84.3 %shard_map.113 = (bf16[2,2,1024,128]{3,2,1,0:T(8,128)(2,1)}, bf16[128,384]{1,0:T(8,128)(2,1)}) custom-call(s32[2]{0:T(128)} %lengths.3, bf16[2,64,32,128]{3,2,1,0:T(8,128)(2,1)} %pair.1, bf16[128,384]{1,0:T(8,128)(2,1)} %bitcast.15, bf16[128,512]{1,0:T(8,128)(2,1)} %bitcast.13, bf16[128,128]{1,0:T(8,128)(2,1)} %bitcast.16, bf16[128,128]{1,0:T(8,128)(2,1)} %bitcast.17, ...), custom_call_target="tpu_custom_call" | custom-call | tf_op jit(solution)/shard_map/pallas_call | solution.py:617
  84.9 2.7 %shard_map.114 = (bf16[1,2,2,1024,128]{4,3,2,1,0:T(8,128)(2,1)}, bf16[128,384]{1,0:T(8,128)(2,1)}) custom-call(s32[2]{0:T(128)} %lengths.3, bf16[2,2,1024,128]{3,2,1,0:T(8,128)(2,1)} %get-tuple-element.6.staged, bf16[128,384]{1,0:T(8,128)(2,1)} %get-tuple-element.7.staged_single), custom_call_target="tpu_custom_call" | custom-call | tf_op jit(solution)/shard_map/pallas_call | solution.py:720
